TPU v7x, 256 devices: a whole 4x4x8 slice. The times are simulated.
256 devices in a mesh: samp: 16 (over x, y_hi, core), var: 8 (over z), row: 2 (over y_lo).
Axes of the slice: x: 4, y: 4 (y_hi: 2, y_lo: 2; y = y_hi * 2 + y_lo), z: 8, core: 2. Of those that a mesh axis runs over, the one named last changes fastest.
Arguments:
- col_dosage: bfloat16 [2, 2048, 8192], P(None, 'var', 'samp'), may hold values from 0 to 1
- col_ancestry: bfloat16 [3, 2, 2048, 8192], P(None, None, 'var', 'samp'), may hold values from 0 to 1, as said below
- row_dosage: bfloat16 [2, 2048, 4096], P(None, 'var', ('row', 'samp')), may hold values from 0 to 1
- row_ancestry: bfloat16 [3, 2, 2048, 4096], P(None, None, 'var', ('row', 'samp')), may hold values from 0 to 1, as said below
Outputs:
- kinship: float32 [4096, 3, 8192], P(('row', 'var'), None, 'samp')
Inputs may be any that keep to these rules, and one draw needn't show every extreme that they name: `col_ancestry`: posteriors are positive and the three of a haplotype sum to at most about one (after rounding to bfloat16); the remainder is the chance that the call is missing. `row_ancestry`: as for col_ancestry.
All inputs are finite; a program needn't handle non-finite values.
Results may differ from a plain program's by a relative error of at most 0.00063.
Values may be sent and summed in bfloat16 or wider, within the bound.
A program may use at most 64 MiB of HBM per device.

v0:
```python
import jax
import jax.numpy as jnp
from jax import lax
from jax.sharding import PartitionSpec as P


def centre(dosage, ancestry, freq):
    values = dosage.astype(jnp.float32)
    shares = ancestry.astype(jnp.float32)
    return jnp.sum(shares * (values[None] - freq[:, None, :, None]), axis=1).astype(jnp.bfloat16)


def local(col_dosage, col_ancestry, row_dosage, row_ancestry):
    values = col_dosage.astype(jnp.float32)
    shares = col_ancestry.astype(jnp.float32)
    local_counts = jnp.sum(shares, axis=(1, 3))
    local_sums = jnp.sum(shares * values[None], axis=(1, 3))
    counts, sums = lax.psum((local_counts, local_sums), "samp")
    freq = sums / counts
    tile_dosage, tile_ancestry = (
        lax.all_gather(row_dosage, "samp", axis=2, tiled=True),
        lax.all_gather(row_ancestry, "samp", axis=3, tiled=True),
    )
    row_centred = centre(tile_dosage, tile_ancestry, freq)
    col_centred = centre(col_dosage, col_ancestry, freq)
    spread = lax.psum(jnp.sum(freq * (1.0 - freq), axis=1), "var")
    total = lax.psum_scatter(
        jnp.einsum("avr,avc->rac", row_centred, col_centred, preferred_element_type=jnp.float32),
        "var",
        scatter_dimension=0,
        tiled=True,
    )
    return total / spread[None, :, None]


def solution(mesh):
    placed = (
        P(None, "var", "samp"),
        P(None, None, "var", "samp"),
        P(None, "var", ("row", "samp")),
        P(None, None, "var", ("row", "samp")),
    )
    return jax.shard_map(
        local,
        mesh=mesh,
        in_specs=placed,
        out_specs=P(("row", "var"), None, "samp"),
        check_vma=False,
    )
```

profile of v0, /device:TPU:1, one launch (start us, length us, event | category | flops | bytes accessed | tf_op | source)
XLA Modules:
  0.0 300.3 jit_solution(8978203238879077094)
XLA Ops:
  6.5 0.0 copy-start
  6.5 0.0 all-gather.5.cloned.1.call-start
  6.5 0.7 all-gather.5.cloned.1.call-update
  7.3 0.0 all-gather.3.cloned.1.call-start
  7.3 0.7 all-gather.3.cloned.1.call-update
  8.0 0.0 reduce-scatter.2.cloned.1.call-start
  8.1 1.2 convert_element_type.21
  9.2 0.0 copy-done
  9.2 0.6 convert_reduce_fusion
  9.9 36.2 %all-reduce = (f32[3,256]{1,0:T(4,128)S(1)}, f32[3,256]{1,0:T(4,128)S(1)}) all-reduce(f32[3,256]{1,0:T(4,128)S(1)} %get-tuple-element.6, f32[3,256]{1,0:T(4,128)S(1)} %get-tuple-element.5), channel_id=1, replica_groups=mesh['samp'=16,'var'=8,'row'=2] {'samp'}, use_global_device_ids=true, to_apply=%region_1.0 | all-reduce | flops 1536 | bytes 12288 | tf_op jit(solution)/shard_map/psum | solution.py:18
  46.1 0.1 fusion.4
  46.2 0.5 fusion.1
  46.7 22.2 %all-gather.5.cloned.1.call-done = bf16[2,256,2048]{2,1,0:T(8,128)(2,1)} async-done(((bf16[2,256,128]{2,1,0:T(8,128)(2,1)}), bf16[2,256,2048]{2,1,0:T(8,128)(2,1)}) %all-gather.5.cloned.1.call-update) | async-done | bytes 2097168 | tf_op jit(solution)/shard_map/all_gather | solution.py:21
  68.8 4.2 %convert_element_type.24 = f32[2,256,2048]{2,1,0:T(8,128)} convert(bf16[2,256,2048]{2,1,0:T(8,128)(2,1)} %all-gather.5.cloned.1.call-done) | non-fusion elementwise | flops 1048576 | bytes 6291456 | tf_op jit(solution)/shard_map/convert_element_type | solution.py:8
  73.0 71.8 %all-gather.3.cloned.1.call-done = bf16[3,2,256,2048]{3,2,1,0:T(8,128)(2,1)} async-done(((bf16[3,2,256,128]{3,2,1,0:T(8,128)(2,1)}), bf16[3,2,256,2048]{3,2,1,0:T(8,128)(2,1)}) %all-gather.3.cloned.1.call-update) | async-done | bytes 6291472 | tf_op jit(solution)/shard_map/all_gather | solution.py:22
  144.8 6.2 %multiply_reduce_fusion = bf16[3,256,2048]{2,1,0:T(8,128)(2,1)S(1)} fusion(bf16[3,2,256,2048]{3,2,1,0:T(8,128)(2,1)} %all-gather.3.cloned.1.call-done, f32[3,256]{1,0:T(4,128)S(1)} %get-tuple-element.10, f32[2,256,2048]{2,1,0:T(8,128)} %convert_element_type.24), kind=kLoop, calls=%fused_computation | loop fusion | flops 11010048 | bytes 13634560 | tf_op jit(solution)/shard_map/reduce_sum | solution.py:10
  151.0 6.4 %convolution_bitcast_fusion = f32[2048,3,512]{0,2,1:T(8,128)} fusion(bf16[3,256,2048]{2,1,0:T(8,128)(2,1)S(1)} %multiply_reduce_fusion, bf16[3,256,512]{2,1,0:T(8,128)(2,1)S(1)} %fusion.1), kind=kOutput, calls=%fused_computation.1 | convolution fusion | flops 1610612736 | bytes 16515072 | tf_op jit(solution)/shard_map/avr,avc->rac/dot_general | solution.py:28
  157.4 0.0 reduce-scatter.2.cloned.1.call-update
  157.5 14.1 %psum.23 = f32[3]{0:T(128)S(1)} all-reduce(f32[3]{0:T(128)S(1)} %get-tuple-element.9), channel_id=1, replica_groups=mesh['samp'=16,'var'=8,'row'=2] {'var'}, use_global_device_ids=true, to_apply=%region_8.0 | all-reduce | flops 3 | bytes 24 | tf_op jit(solution)/shard_map/psum | solution.py:26
  171.6 118.9 %reduce-scatter.2.cloned.1.call-done = f32[256,3,512]{0,2,1:T(8,128)} async-done(((f32[2048,3,512]{0,2,1:T(8,128)}), f32[256,3,512]{0,2,1:T(8,128)}) %reduce-scatter.2.cloned.1.call-update) | async-done | bytes 1572880 | tf_op jit(solution)/shard_map/reduce_scatter | solution.py:27
  290.5 1.6 broadcast_divide_fusion
  292.2 1.6 copy.7
Async XLA Ops:
  6.5 2.7 copy-start
  6.5 62.3 %all-gather.5.cloned.1.call-start = ((), (), s32[]{:S(2)}) async-start(), calls=%async_computation.2 | async-start | bytes 2228224 | tf_op jit(solution)/shard_map/all_gather | solution.py:21
  7.3 137.5 %all-gather.3.cloned.1.call-start = ((), (), s32[]{:S(2)}) async-start(), calls=%async_computation.1 | async-start | bytes 6684672 | tf_op jit(solution)/shard_map/all_gather | solution.py:22
  8.0 282.5 %reduce-scatter.2.cloned.1.call-start = ((), (), s32[]{:S(2)}) async-start(), calls=%async_computation.3 | async-start | bytes 14155776 | tf_op jit(solution)/shard_map/reduce_scatter | solution.py:27
Sparse Core Ops, SparseCore 0:
  9.9 58.8 all-gather.4
  71.4 73.3 all-gather.2
  157.6 132.9 reduce-scatter.1
where the time goes:
time: 301 us; the launch traced here: 300 us
  waiting for transfers between devices  214 us (71%)
  blocking collectives  50.4 us (17%)
  other arithmetic  14.4 us (5%)
  between operations  13.2 us (4%)
  matrix products  6.43 us (2%)
    reduce_scatter x1, waiting for transfers between devices, local(): lax.psum_scatter(jnp.einsum('avr,avc->rac', row_centred, col_centred, pre...  119 us
    all_gather x1, waiting for transfers between devices, local(): lax.all_gather(row_ancestry, 'samp', axis=3, tiled=True)  71.8 us
    psum x1, blocking collectives, local(): counts, sums = lax.psum((local_counts, local_sums), 'samp')  36.2 us
    all_gather x1, waiting for transfers between devices, local(): lax.all_gather(row_dosage, 'samp', axis=2, tiled=True)  22.2 us
    psum x1, blocking collectives, local(): spread = lax.psum(jnp.sum(freq * (1.0 - freq), axis=1), 'var')  14.1 us
    reduce_sum x2, other arithmetic, centre(): jnp.sum(shares * (values[None] - freq[:, None, :, None]), axis=1)  6.67 us
    dot_general x1, matrix products, local(): jnp.einsum('avr,avc->rac', row_centred, col_centred, preferred_element_ty...  6.43 us
  transfers between devices with their start and end apart: 3, of which 3 were waited for; matrix products, arithmetic and copies ran while one was open for 2% of the time, Pallas kernels for 0%

commit v1 on v0

v1 whole, which is shorter than its diff:
```python
import functools

import jax
import jax.numpy as jnp
from jax import lax
from jax.experimental import pallas as pl
from jax.experimental.pallas import tpu as pltpu
from jax.sharding import PartitionSpec as P

MESH = pl.DeviceIdType.MESH
F32 = jnp.float32
BF16 = jnp.bfloat16
HALVES = 2


def device(s, z, r):
    return {"samp": s, "var": z, "row": r}


def aligned(value, size):
    return pl.multiple_of(value, size)


def kernel(
    sizes,
    cd_hbm,
    ca_hbm,
    rd_hbm,
    ra_hbm,
    out_hbm,
    spread_ref,
    cd,
    ca,
    rd,
    ra,
    pst,
    stat,
    freq,
    spreads,
    rows_t,
    a_buf,
    b_buf,
    c_send,
    c_recv,
    o_buf,
    in_sem,
    out_sem,
    stat_send,
    stat_recv,
    spread_send,
    spread_recv,
    t_send,
    t_recv,
    g_send,
    g_recv,
    f_send,
    f_recv,
    b_send,
    b_recv,
    c_ssem,
    c_rsem,
):
    ns, nz, nr = sizes
    np_ = ns // 2
    s, z, r = lax.axis_index("samp"), lax.axis_index("var"), lax.axis_index("row")
    p, c = s // 2, s % 2
    sib = s + 1 - 2 * c
    other = 1 - r
    na = ca.shape[0]
    nv = cd.shape[1]
    kv = nv // nr
    cols = cd.shape[2]
    wide = cols // HALVES
    chunks = na * HALVES
    piece = 128 // np_

    loads = [
        pltpu.make_async_copy(src, dst, in_sem.at[i])
        for i, (src, dst) in enumerate(((cd_hbm, cd), (ca_hbm, ca), (rd_hbm, rd), (ra_hbm, ra)))
    ]
    for load in loads:
        load.start()

    barrier = pltpu.get_barrier_semaphore()

    def greet(who):
        pl.semaphore_signal(barrier, inc=1, device_id=who, device_id_type=MESH)

    for i in range(1, ns):
        greet(device((s + i) % ns, z, r))
    for i in range(1, nz):
        greet(device(s, (z + i) % nz, r))
    greet(device(s, z, other))
    for k in range(nz):
        for ry in range(nr):
            own = (p == z) & (k == z) & (ry == r)

            @pl.when(jnp.logical_not(own))
            def _():
                greet(device(z * 2 + c, k, ry))

    loads[0].wait()
    loads[1].wait()
    step = 32

    def fold(x):
        total = x[:, :128]
        for t in range(1, cols // 128):
            total = total + x[:, t * 128:(t + 1) * 128]
        return total

    def stats(i, carry):
        rows = pl.ds(aligned(i * step, step), step)
        dosage = [cd[h, rows, :].astype(F32) for h in range(2)]
        for a in range(na):
            share = [ca[a, h, rows, :].astype(F32) for h in range(2)]
            pst[a, rows, :] = fold(share[0] + share[1])
            pst[4 + a, rows, :] = fold(share[0] * dosage[0] + share[1] * dosage[1])
        return carry

    lax.fori_loop(0, nv // step, stats, 0)
    for a in range(na):
        for k in (a, 4 + a):
            stat[s, k:k + 1, :] = jnp.sum(pst[k].T, axis=0, keepdims=True)
    for k in (3, 7):
        stat[s, k:k + 1, :] = jnp.ones((1, nv), F32)

    pl.semaphore_wait(barrier, (ns - 1) + (nz - 1) + 1 + nz * nr - jnp.where(p == z, 1, 0))

    sent = []

    def push(src, dst, send_sem, recv_sem, who):
        copy = pltpu.make_async_remote_copy(
            src_ref=src, dst_ref=dst, send_sem=send_sem, recv_sem=recv_sem, device_id=who, device_id_type=MESH
        )
        copy.start()
        sent.append(copy)

    def arrive(dst, sem):
        pltpu.make_async_copy(dst, dst, sem).wait()

    for i in range(1, ns):
        push(stat.at[s], stat.at[s], stat_send.at[i], stat_recv.at[i], device((s + i) % ns, z, r))
    for i in range(1, ns):
        arrive(stat.at[(s + ns - i) % ns], stat_recv.at[i])
    total = stat[0]
    for i in range(1, ns):
        total = total + stat[i]
    ratio = total[4:8] / total[0:4]
    spreads[z, 0:4, :] = jnp.broadcast_to(jnp.sum(ratio * (1.0 - ratio), axis=1, keepdims=True), (4, 128))
    spreads[z, 4:8, :] = jnp.zeros((4, 128), F32)
    for a in range(na):
        freq[a] = jnp.broadcast_to(ratio[a:a + 1, :], (128, nv)).T

    loads[2].wait()
    loads[3].wait()
    for a in range(na):
        centred = ra[a, 0].astype(F32) * (rd[0].astype(F32) - freq[a])
        centred = centred + ra[a, 1].astype(F32) * (rd[1].astype(F32) - freq[a])
        turned = centred.T.astype(BF16)
        for k in range(nr):
            rows_t[a, k] = turned[:, k * kv:(k + 1) * kv]

    def block(ry, core, e, zz):
        return a_buf.at[:, ry, pl.ds(aligned(core * 128 + e * piece, piece), piece), pl.ds(aligned(zz * kv, kv), kv)]

    for e in range(np_):
        for k in range(nr):
            src = rows_t.at[:, k, pl.ds(e * piece, piece), :]
            own = (p == e) & (p == z) & (k == r)
            number = e * nr + k

            @pl.when(own)
            def _():
                pltpu.make_async_copy(src, block(r, c, p, z), t_recv.at[z * nr + r]).start()

            @pl.when(jnp.logical_not(own))
            def _():
                pltpu.make_async_remote_copy(
                    src_ref=src,
                    dst_ref=block(r, c, e, z),
                    send_sem=t_send.at[number],
                    recv_sem=t_recv.at[z * nr + r],
                    device_id=device(e * 2 + c, p, k),
                    device_id_type=MESH,
                ).start()

    def centre(a):
        def part(i, carry):
            at = pl.ds(aligned(r * kv + i * step, step), step)
            to = pl.ds(aligned(z * kv + i * step, step), step)
            f = freq[a, at, :]
            f = jnp.concatenate([f] * (wide // 128), axis=1)
            for half in range(HALVES):
                lanes = pl.ds(half * wide, wide)
                value = ca[a, 0, at, lanes].astype(F32) * (cd[0, at, lanes].astype(F32) - f)
                value = value + ca[a, 1, at, lanes].astype(F32) * (cd[1, at, lanes].astype(F32) - f)
                b_buf[a * HALVES + half, to, :] = value.astype(BF16)
            return carry

        lax.fori_loop(0, kv // step, part, 0)

    def b_rows(j, zz, first=0, count=None):
        count = kv if count is None else count
        return b_buf.at[j, pl.ds(aligned(zz * kv + first, 64), count), :]

    far = nz // 2
    ways = (1, nz - 1)

    def b_part(j, zz, way, d):
        if d == far:
            return b_rows(j, zz, way * (kv // 2), kv // 2)
        return b_rows(j, zz)

    def b_move(j, way, d):
        origin = (z + (nz - ways[way]) * (d - 1)) % nz
        ref = b_part(j, origin, way, d)
        push(ref, ref, b_send.at[j, way, d - 1], b_recv.at[j, way, d - 1], device(s, (z + ways[way]) % nz, r))

    def b_arrive(j, way, d):
        origin = (z + (nz - ways[way]) * d) % nz
        arrive(b_part(j, origin, way, d), b_recv.at[j, way, d - 1])

    def a_piece(a, core, e):
        return a_buf.at[a, :, pl.ds(aligned(core * 128 + e * piece, piece), piece), :]

    def a_spread(a):
        for i in range(1, np_):
            q = (p + i) % np_
            push(a_piece(a, c, p), a_piece(a, c, p), g_send.at[a, i], g_recv.at[a, i], device(q * 2 + c, z, r))
        push(a_piece(a, c, p), a_piece(a, c, p), f_send.at[a, 0], f_recv.at[a, 0], device(sib, z, r))

    def a_collect(a):
        for i in range(1, np_):
            q = (p + np_ - i) % np_
            arrive(a_piece(a, c, q), g_recv.at[a, i])
            push(a_piece(a, c, q), a_piece(a, c, q), f_send.at[a, i], f_recv.at[a, i], device(sib, z, r))
        for i in range(np_):
            q = (p + np_ - i) % np_
            arrive(a_piece(a, 1 - c, q), f_recv.at[a, i])

    def multiply(j):
        a, half = j // HALVES, j % HALVES
        b = b_buf[j]
        c_send[j] = jnp.dot(a_buf[a, other], b, preferred_element_type=F32)
        push(c_send.at[j], c_recv.at[j], c_ssem.at[j], c_rsem.at[j], device(s, z, other))
        o_buf[a, :, pl.ds(half * wide, wide)] = jnp.dot(a_buf[a, r], b, preferred_element_type=F32)

    stores = []

    def finish(j):
        a, half = j // HALVES, j % HALVES
        arrive(c_recv.at[j], c_rsem.at[j])
        o_buf[a, :, pl.ds(half * wide, wide)] += c_recv[j]
        if half == HALVES - 1:
            store = pltpu.make_async_copy(o_buf.at[a], out_hbm.at[a], out_sem.at[a])
            store.start()
            stores.append(store)

    def launch(pair):
        for j in pair:
            for way in range(2):
                b_move(j, way, 1)

    pairs = [tuple(range(a * HALVES, (a + 1) * HALVES)) for a in range(na)]
    lead = far - 1
    for tick in range(lead * (na - 1) + far + 1):
        for a, pair in enumerate(pairs):
            d = tick - lead * a
            if d == 0:
                if tick == 0:
                    centre(a)
                launch(pair)
            elif 1 <= d <= far:
                for j in pair:
                    for way in range(2):
                        b_arrive(j, way, d)
                        if d < far:
                            b_move(j, way, d + 1)
                if d == far:
                    for j in pair:
                        multiply(j)
                    if a > 0:
                        for j in pairs[a - 1]:
                            finish(j)
        if tick == 0:
            for i in range(1, nz):
                push(
                    spreads.at[z], spreads.at[z], spread_send.at[i], spread_recv.at[i], device(s, (z + i) % nz, r)
                )
            for zz in range(nz):
                for ry in range(nr):
                    arrive(block(ry, c, p, zz), t_recv.at[zz * nr + ry])
            for a in range(na):
                a_spread(a)
            for a in range(1, na):
                centre(a)
        if tick >= 1 and tick % 2 == 1 and tick // 2 < na:
            a_collect(tick // 2)
    for i in range(1, nz):
        arrive(spreads.at[(z + nz - i) % nz], spread_recv.at[i])
    spread = spreads[0]
    for i in range(1, nz):
        spread = spread + spreads[i]
    spread_ref[...] = spread
    for j in pairs[-1]:
        finish(j)

    for e in range(np_):
        for k in range(nr):
            own = (p == e) & (p == z) & (k == r)
            src = rows_t.at[:, k, pl.ds(e * piece, piece), :]

            @pl.when(jnp.logical_not(own))
            def _():
                pltpu.make_async_copy(src, src, t_send.at[e * nr + k]).wait()

    for copy in sent:
        copy.wait_send()
    for store in stores:
        store.wait()


def local(sizes, col_dosage, col_ancestry, row_dosage, row_ancestry):
    ns, nz, nr = sizes
    np_ = ns // 2
    na = col_ancestry.shape[0]
    nv, cols = col_dosage.shape[1:]
    rows = row_dosage.shape[2]
    kv = nv // nr
    tall = 2 * rows
    wide = cols // HALVES
    chunks = na * HALVES
    far = nz // 2
    dma = pltpu.SemaphoreType.DMA
    total, spread = pl.pallas_call(
        functools.partial(kernel, sizes),
        out_shape=(
            jax.ShapeDtypeStruct((na, tall, cols), F32),
            jax.ShapeDtypeStruct((8, 128), F32),
        ),
        in_specs=[pl.BlockSpec(memory_space=pl.ANY)] * 4,
        out_specs=(pl.BlockSpec(memory_space=pl.ANY), pl.BlockSpec(memory_space=pltpu.VMEM)),
        scratch_shapes=[
            pltpu.VMEM(col_dosage.shape, BF16),
            pltpu.VMEM(col_ancestry.shape, BF16),
            pltpu.VMEM(row_dosage.shape, BF16),
            pltpu.VMEM(row_ancestry.shape, BF16),
            pltpu.VMEM((8, nv, 128), F32),
            pltpu.VMEM((ns, 8, nv), F32),
            pltpu.VMEM((na, nv, 128), F32),
            pltpu.VMEM((nz, 8, 128), F32),
            pltpu.VMEM((na, nr, rows, kv), BF16),
            pltpu.VMEM((na, nr, tall, nz * kv), BF16),
            pltpu.VMEM((chunks, nz * kv, wide), BF16),
            pltpu.VMEM((chunks, tall, wide), F32),
            pltpu.VMEM((chunks, tall, wide), F32),
            pltpu.VMEM((na, tall, cols), F32),
            dma((4,)),
            dma((na,)),
            dma((ns,)),
            dma((ns,)),
            dma((nz,)),
            dma((nz,)),
            dma((np_ * nr,)),
            dma((nz * nr,)),
            dma((na, np_)),
            dma((na, np_)),
            dma((na, np_)),
            dma((na, np_)),
            dma((chunks, 2, far)),
            dma((chunks, 2, far)),
            dma((chunks,)),
            dma((chunks,)),
        ],
        compiler_params=pltpu.CompilerParams(
            collective_id=0, has_side_effects=True, vmem_limit_bytes=48 * 1024 * 1024
        ),
    )(col_dosage, col_ancestry, row_dosage, row_ancestry)
    return jnp.transpose(total / spread[:na, :1][:, :, None], (1, 0, 2))


def solution(mesh):
    sizes = (mesh.shape["samp"], mesh.shape["var"], mesh.shape["row"])
    placed = (
        P(None, "var", "samp"),
        P(None, None, "var", "samp"),
        P(None, "var", ("row", "samp")),
        P(None, None, "var", ("row", "samp")),
    )
    return jax.shard_map(
        functools.partial(local, sizes),
        mesh=mesh,
        in_specs=placed,
        out_specs=P(("row", "var"), None, "samp"),
        check_vma=False,
    )
```

time: 301 us -> 104 us (0.35)
  the two profiles are of different devices: /device:TPU:1 before, /device:TPU:30 now
where the time goes in v1:
time: 104 us
  Pallas kernels  97.6 us (94%)
  local copies, waits for them, and re-layouts  4.46 us (4%)
  other arithmetic  1.43 us (1%)
    pallas_call x1, Pallas kernels, local(): pl.pallas_call(functools.partial(kernel, sizes), out_shape=(jax.ShapeDtyp...  97.6 us
    unnamed x8, local copies, waits for them, and re-layouts  4.35 us

profile of v1, /device:TPU:30, one launch (start us, length us, event | category | flops | bytes accessed | tf_op | source)
XLA Modules:
  0.0 103.5 jit_solution(9289433108398266006)
XLA Ops:
  0.0 0.0 copy-start
  0.0 1.4 %copy-done = bf16[3,2,256,512]{3,2,1,0:T(8,128)(2,1)S(1)} copy-done((bf16[3,2,256,512]{3,2,1,0:T(8,128)(2,1)S(1)}, bf16[3,2,256,512]{3,2,1,0:T(8,128)(2,1)}, u32[]{:S(2)}) %copy-start) | copy-done | bytes 1572888
  1.4 0.0 copy-start.1
  1.4 1.0 %copy-done.1 = bf16[2,256,512]{2,1,0:T(8,128)(2,1)S(1)} copy-done((bf16[2,256,512]{2,1,0:T(8,128)(2,1)S(1)}, bf16[2,256,512]{2,1,0:T(8,128)(2,1)}, u32[]{:S(2)}) %copy-start.1) | copy-done | bytes 524312
  2.5 0.0 copy-start.2
  2.5 1.0 copy-done.2
  3.4 0.0 copy-start.3
  3.4 0.9 copy-done.3
  4.4 97.6 %shard_map.46 = (f32[3,256,512]{2,1,0:T(8,128)S(1)}, f32[8,128]{1,0:T(8,128)S(1)}) custom-call(bf16[2,256,512]{2,1,0:T(8,128)(2,1)S(1)} %copy-done.1, bf16[3,2,256,512]{3,2,1,0:T(8,128)(2,1)S(1)} %copy-done, bf16[2,256,128]{2,1,0:T(8,128)(2,1)S(1)} %copy-done.3, bf16[3,2,256,128]{3,2,1,0:T(8,128)(2,1)S(1)} %copy-done.2), custom_call_target="tpu_custom_call" | custom-call | tf_op jit(solution)/shard_map/pallas_call | solution.py:336
  102.0 0.1 slice_reduce_fusion
  102.1 1.4 %divide_bitcast_fusion = f32[256,3,512]{2,0,1:T(8,128)} fusion(f32[3,256,512]{2,1,0:T(8,128)S(1)} %get-tuple-element.7, f32[3]{0:T(128)S(1)} %slice_reduce_fusion), kind=kLoop, calls=%fused_computation | loop fusion | flops 393216 | bytes 3145740 | tf_op jit(solution)/shard_map/transpose | solution.py:380
Async XLA Ops:
  0.0 1.4 %copy-start = (bf16[3,2,256,512]{3,2,1,0:T(8,128)(2,1)S(1)}, bf16[3,2,256,512]{3,2,1,0:T(8,128)(2,1)}, u32[]{:S(2)}) copy-start(bf16[3,2,256,512]{3,2,1,0:T(8,128)(2,1)} %ca_hbm.1) | copy-start | bytes 4718596
  1.4 1.0 %copy-start.1 = (bf16[2,256,512]{2,1,0:T(8,128)(2,1)S(1)}, bf16[2,256,512]{2,1,0:T(8,128)(2,1)}, u32[]{:S(2)}) copy-start(bf16[2,256,512]{2,1,0:T(8,128)(2,1)} %cd_hbm.1) | copy-start | bytes 1572868
  2.5 1.0 copy-start.2
  3.4 0.9 copy-start.3

commit v2 on v0

v2 whole, which is shorter than its diff:
```python
import functools

import jax
import jax.numpy as jnp
from jax import lax
from jax.experimental import pallas as pl
from jax.experimental.pallas import tpu as pltpu
from jax.sharding import PartitionSpec as P

MESH = pl.DeviceIdType.MESH
F32 = jnp.float32
BF16 = jnp.bfloat16
HALVES = 2
STEP = 32


def device(s, z, r):
    return {"samp": s, "var": z, "row": r}


def aligned(value, size):
    return pl.multiple_of(value, size)


def kernel(
    sizes,
    cd_hbm,
    ca_hbm,
    rd_hbm,
    ra_hbm,
    out_ref,
    spread_ref,
    cd,
    ca,
    rd,
    ra,
    pst,
    part,
    stat,
    ratios,
    freq,
    spreads,
    turned,
    raw,
    centred,
    hold,
    a_buf,
    a_far,
    b_buf,
    c_send,
    c_recv,
    o_buf,
    in_sem,
    out_sem,
    pair_sem,
    stat_sem,
    spread_sem,
    t1_sem,
    t2_sem,
    g1_sem,
    g2_sem,
    f_sem,
    far_sem,
    b_sem,
    c_sem,
):
    ns, nz, nr = sizes
    nx, np_ = ns // 4, ns // 2
    s, z, r = lax.axis_index("samp"), lax.axis_index("var"), lax.axis_index("row")
    x, h, c = s // 4, (s // 2) % 2, s % 2
    p = s // 2
    other = 1 - r
    na = ca.shape[0]
    nv, cols = cd.shape[1:]
    kv = nv // nr
    wide = cols // HALVES
    piece = rd.shape[2] // np_
    far = nz // 2
    sibling = device(s + 1 - 2 * c, z, r)
    mate = device(s, z, other)
    across = device((x * 2 + 1 - h) * 2 + c, z, other)

    def chip(q):
        return q * 2 + c

    loads = [
        pltpu.make_async_copy(src, dst, in_sem.at[i])
        for i, (src, dst) in enumerate(((cd_hbm, cd), (ca_hbm, ca), (rd_hbm, rd), (ra_hbm, ra)))
    ]
    for load in loads:
        load.start()

    barrier = pltpu.get_barrier_semaphore()

    def greet(who):
        pl.semaphore_signal(barrier, inc=1, device_id=who, device_id_type=MESH)

    greet(sibling)
    for i in range(1, nz):
        greet(device(s, (z + i) % nz, r))
    for i in range(np_):
        for k in range(nr):
            if i or k:
                greet(device(chip((p + i) % np_), z, (r + k) % nr))

    loads[0].wait()
    loads[1].wait()

    def fold(value):
        total = value[:, :128]
        for t in range(1, cols // 128):
            total = total + value[:, t * 128:(t + 1) * 128]
        return total

    def stats(i, carry):
        rows = pl.ds(aligned(i * STEP, STEP), STEP)
        dosage = [cd[k, rows, :].astype(F32) for k in range(2)]
        for a in range(na):
            share = [ca[a, k, rows, :].astype(F32) for k in range(2)]
            pst[a, rows, :] = fold(share[0] + share[1])
            pst[4 + a, rows, :] = fold(share[0] * dosage[0] + share[1] * dosage[1])
        return carry

    lax.fori_loop(0, nv // STEP, stats, 0)
    for a in range(na):
        for k in (a, 4 + a):
            part[c, k:k + 1, :] = jnp.sum(pst[k].T, axis=0, keepdims=True)
    for k in (3, 7):
        part[c, k:k + 1, :] = jnp.ones((1, nv), F32)

    pl.semaphore_wait(barrier, 1 + (nz - 1) + np_ * nr - 1)

    sent = []

    def push(src, dst, sems, who):
        copy = pltpu.make_async_remote_copy(
            src_ref=src, dst_ref=dst, send_sem=sems[0], recv_sem=sems[1], device_id=who, device_id_type=MESH
        )
        copy.start()
        sent.append(copy)

    def pair(ref, *at):
        return ref.at[(0, *at)], ref.at[(1, *at)]

    def arrive(dst, sems):
        pltpu.make_async_copy(dst, dst, sems[1]).wait()

    push(part.at[c], part.at[c], pair(pair_sem, 0), sibling)

    loads[2].wait()
    loads[3].wait()
    for k in range(2):
        turned[k] = rd[k].astype(F32).T.astype(BF16)
        for a in range(na):
            turned[2 + 2 * a + k] = ra[a, k].astype(F32).T.astype(BF16)

    arrive(part.at[1 - c], pair(pair_sem, 0))
    stat[p] = part[0] + part[1]
    for i in range(1, nx):
        push(stat.at[p], stat.at[p], pair(stat_sem, 0, i), device(chip(((x + i) % nx) * 2 + h), z, r))
    for i in range(nx):
        push(stat.at[p], stat.at[p], pair(stat_sem, 1, i), device(chip(((x + i) % nx) * 2 + 1 - h), z, other))

    def t1_piece(i, k):
        rows = pl.ds(aligned(((p + i) % np_) * piece, piece), piece)
        half = pl.ds(aligned((1 - (r + k) % nr) * kv, kv), kv)
        return turned.at[:, rows, half], raw.at[:, p, r]

    own = pltpu.make_async_copy(*t1_piece(0, 0), t1_sem.at[1, 0, 0])
    own.start()
    for i in range(np_):
        for k in range(nr):
            if i or k:
                push(*t1_piece(i, k), pair(t1_sem, i, k), device(chip((p + i) % np_), z, (r + k) % nr))

    for i in range(1, nx):
        arrive(stat.at[((x + nx - i) % nx) * 2 + h], pair(stat_sem, 0, i))
    for i in range(nx):
        arrive(stat.at[((x + nx - i) % nx) * 2 + 1 - h], pair(stat_sem, 1, i))
    total = stat[0]
    for i in range(1, np_):
        total = total + stat[i]
    ratio = total[4:8] / total[0:4]
    ratios[0:4, :] = ratio
    for a in range(na):
        freq[a] = jnp.broadcast_to(ratio[a:a + 1, :], (128, nv)).T

    for i in range(np_):
        for k in range(nr):
            arrive(raw.at[:, (p + np_ - i) % np_, (r + nr - k) % nr], pair(t1_sem, i, k))

    def centre_rows(a):
        f = ratios[a:a + 1, pl.ds(aligned(other * kv, kv), kv)]
        f = jnp.broadcast_to(f, (piece, kv))[None, None]
        value = raw[2 + 2 * a].astype(F32) * (raw[0].astype(F32) - f)
        value = value + raw[3 + 2 * a].astype(F32) * (raw[1].astype(F32) - f)
        centred[a] = value.astype(BF16)
        hold[a, :, :, pl.ds(aligned(z * kv, kv), kv)] = centred[a, z]

    def hold_from(a, zz):
        return hold.at[a, :, :, pl.ds(aligned(zz * kv, kv), kv)]

    def t2_send(a):
        for i in range(1, nz):
            to = (z + i) % nz
            push(centred.at[a, to], hold_from(a, z), pair(t2_sem, a, i), device(s, to, r))

    def a_rows(a, ry, core, first, count):
        return a_buf.at[a, ry, pl.ds(aligned(core * 128 + first * piece, piece), count * piece), :]

    def t2_wait(a):
        for i in range(1, nz):
            arrive(hold_from(a, (z + nz - i) % nz), pair(t2_sem, a, i))

    def g1_send(a, o):
        ry = r if o == 0 else other
        for k, who in enumerate((mate, across)):
            push(hold.at[a, ry], a_rows(a, ry, c, p, 1), pair(g1_sem, a, o, k), who)

    def g1_wait(a, o):
        ry = other if o == 0 else r
        arrive(a_rows(a, ry, c, p, 1), pair(g1_sem, a, o, 0))
        arrive(a_rows(a, ry, c, x * 2 + 1 - h, 1), pair(g1_sem, a, o, 1))

    def g2_send(a, o):
        ry = other if o == 0 else r
        ref = a_rows(a, ry, c, x * 2, 2)
        for i in range(1, nx):
            push(ref, ref, pair(g2_sem, a, o, i), device(chip(((x + i) % nx) * 2 + h), z, r))
        push(ref, ref, pair(f_sem, a, o, 0), sibling)

    def g2_wait(a, o):
        ry = other if o == 0 else r
        for i in range(1, nx):
            ref = a_rows(a, ry, c, ((x + nx - i) % nx) * 2, 2)
            arrive(ref, pair(g2_sem, a, o, i))
            push(ref, ref, pair(f_sem, a, o, i), sibling)

    def f_wait(a, o):
        ry = other if o == 0 else r
        for i in range(nx):
            arrive(a_rows(a, ry, 1 - c, ((x + nx - i) % nx) * 2, 2), pair(f_sem, a, o, i))

    def far_rows(core):
        return pl.ds(aligned(core * 128, 128), 128)

    def far_send():
        push(a_buf.at[na - 1, other, far_rows(c)], a_far.at[far_rows(c)], pair(far_sem, 0), across)

    def far_wait():
        arrive(a_far.at[far_rows(c)], pair(far_sem, 0))
        push(a_far.at[far_rows(c)], a_far.at[far_rows(c)], pair(far_sem, 1), sibling)
        arrive(a_far.at[far_rows(1 - c)], pair(far_sem, 1))

    chunks = [(a, half, False) for a in range(na) for half in range(HALVES)]
    both = [(na - 1, HALVES - 1)]
    chunks += [(a, half, True) for a, half in both]
    handed = [j for j, (a, half, extra) in enumerate(chunks) if (a, half) not in both]

    def centre_cols(j):
        a, half, extra = chunks[j]
        first = (other if extra else r) * kv
        lanes = pl.ds(half * wide, wide)

        def body(i, carry):
            at = pl.ds(aligned(first + i * STEP, STEP), STEP)
            to = pl.ds(aligned(z * kv + i * STEP, STEP), STEP)
            f = freq[a, at, :]
            f = jnp.concatenate([f] * (wide // 128), axis=1)
            value = ca[a, 0, at, lanes].astype(F32) * (cd[0, at, lanes].astype(F32) - f)
            value = value + ca[a, 1, at, lanes].astype(F32) * (cd[1, at, lanes].astype(F32) - f)
            b_buf[j, to, :] = value.astype(BF16)
            return carry

        lax.fori_loop(0, kv // STEP, body, 0)

    ways = (1, nz - 1)

    def b_part(j, zz, way, d):
        first, count = (way * (kv // 2), kv // 2) if d == far else (0, kv)
        return b_buf.at[j, pl.ds(aligned(zz * kv + first, 64), count), :]

    def b_move(j, way, d):
        ref = b_part(j, (z + (nz - ways[way]) * (d - 1)) % nz, way, d)
        push(ref, ref, pair(b_sem, j, way, d - 1), device(s, (z + ways[way]) % nz, r))

    def launch(j):
        for way in range(2):
            b_move(j, way, 1)

    def hop(j, d):
        for way in range(2):
            arrive(b_part(j, (z + (nz - ways[way]) * d) % nz, way, d), pair(b_sem, j, way, d - 1))
            if d < far:
                b_move(j, way, d + 1)

    def hand_over(j):
        a = chunks[j][0]
        c_send[j] = jnp.dot(a_buf[a, other], b_buf[j], preferred_element_type=F32)
        push(c_send.at[j], c_recv.at[j], pair(c_sem, j), mate)

    def out_lanes(j):
        return pl.ds(chunks[j][1] * wide, wide)

    def keep(j):
        a = chunks[j][0]
        o_buf[a, :, out_lanes(j)] = jnp.dot(a_buf[a, r], b_buf[j], preferred_element_type=F32)

    stores = []

    def store(j):
        a = chunks[j][0]
        copy = pltpu.make_async_copy(o_buf.at[a, :, out_lanes(j)], out_ref.at[a, :, out_lanes(j)], out_sem.at[j])
        copy.start()
        stores.append(copy)

    def finish(j):
        a = chunks[j][0]
        arrive(c_recv.at[j], pair(c_sem, j))
        o_buf[a, :, out_lanes(j)] += c_recv[j]
        store(j)

    centre_rows(0)
    t2_send(0)
    for j in range(2):
        centre_cols(j)
        launch(j)
    centre_cols(2)
    launch(2)
    for a in range(1, na):
        centre_rows(a)
        t2_send(a)
    spreads[z, 0:4, :] = jnp.broadcast_to(jnp.sum(ratio * (1.0 - ratio), axis=1, keepdims=True), (4, 128))
    spreads[z, 4:8, :] = jnp.zeros((4, 128), F32)
    for i in range(1, nz):
        push(spreads.at[z], spreads.at[z], pair(spread_sem, i), device(s, (z + i) % nz, r))
    for j in range(3, len(chunks)):
        centre_cols(j)

    hop(0, 1)
    t2_wait(0)
    g1_send(0, 0)
    g1_send(0, 1)
    hop(1, 1)
    hop(2, 1)
    for a in range(1, na):
        t2_wait(a)
        g1_send(a, 0)
        g1_send(a, 1)
    hop(0, 2)
    hop(1, 2)
    g1_wait(0, 0)
    g2_send(0, 0)
    g1_wait(0, 1)
    g2_send(0, 1)
    hop(2, 2)
    for a in range(1, na):
        for o in range(2):
            g1_wait(a, o)
            g2_send(a, o)
    hop(0, 3)
    launch(3)
    hop(1, 3)
    launch(4)
    hop(2, 3)
    launch(5)
    g2_wait(0, 0)
    f_wait(0, 0)
    hop(0, 4)
    hand_over(0)
    launch(6)
    hop(1, 4)
    hand_over(1)
    g2_wait(1, 0)
    hop(3, 1)
    hop(2, 4)
    f_wait(1, 0)
    hand_over(2)
    hop(4, 1)
    hop(5, 1)
    hop(6, 1)
    g2_wait(0, 1)
    f_wait(0, 1)
    keep(0)
    keep(1)
    hop(3, 2)
    g2_wait(1, 1)
    g2_wait(2, 0)
    f_wait(1, 1)
    keep(2)
    hop(4, 2)
    hop(5, 2)
    g2_wait(2, 1)
    f_wait(2, 0)
    f_wait(2, 1)
    far_send()
    hop(6, 2)
    finish(0)
    hop(3, 3)
    hop(4, 3)
    hop(5, 3)
    far_wait()
    hop(6, 3)
    finish(1)
    hop(3, 4)
    hand_over(3)
    keep(3)
    hop(4, 4)
    hand_over(4)
    keep(4)
    finish(2)
    hop(5, 4)
    hop(6, 4)
    a, lanes = chunks[5][0], out_lanes(5)
    o_buf[a, :, lanes] = jnp.dot(a_buf[a, r], b_buf[5], preferred_element_type=F32)
    o_buf[a, :, lanes] += jnp.dot(a_far[...], b_buf[6], preferred_element_type=F32)
    store(5)

    for i in range(1, nz):
        arrive(spreads.at[(z + nz - i) % nz], pair(spread_sem, i))
    spread = spreads[0]
    for i in range(1, nz):
        spread = spread + spreads[i]
    for a in range(na):
        spread_ref[a:a + 1, :] = jnp.concatenate([spread[a:a + 1, :]] * (cols // 128), axis=1)
    for j in handed[3:]:
        finish(j)

    for copy in sent:
        copy.wait_send()
    for copy in stores:
        copy.wait()


def local(sizes, col_dosage, col_ancestry, row_dosage, row_ancestry):
    ns, nz, nr = sizes
    nx, np_ = ns // 4, ns // 2
    na = col_ancestry.shape[0]
    nv, cols = col_dosage.shape[1:]
    rows = row_dosage.shape[2]
    kv = nv // nr
    tall = 2 * rows
    wide = cols // HALVES
    piece = rows // np_
    chunks = na * HALVES + 1
    far = nz // 2
    dma = pltpu.SemaphoreType.DMA
    total, spread = pl.pallas_call(
        functools.partial(kernel, sizes),
        out_shape=(
            jax.ShapeDtypeStruct((na, tall, cols), F32),
            jax.ShapeDtypeStruct((na, cols), F32),
        ),
        in_specs=[pl.BlockSpec(memory_space=pltpu.HBM)] * 4,
        out_specs=(pl.BlockSpec(memory_space=pl.ANY), pl.BlockSpec(memory_space=pltpu.VMEM)),
        scratch_shapes=[
            pltpu.VMEM(col_dosage.shape, BF16),
            pltpu.VMEM(col_ancestry.shape, BF16),
            pltpu.VMEM(row_dosage.shape, BF16),
            pltpu.VMEM(row_ancestry.shape, BF16),
            pltpu.VMEM((8, nv, 128), F32),
            pltpu.VMEM((2, 8, nv), F32),
            pltpu.VMEM((np_, 8, nv), F32),
            pltpu.VMEM((8, nv), F32),
            pltpu.VMEM((na, nv, 128), F32),
            pltpu.VMEM((nz, 8, 128), F32),
            pltpu.VMEM((2 + 2 * na, rows, nv), BF16),
            pltpu.VMEM((2 + 2 * na, np_, nr, piece, kv), BF16),
            pltpu.VMEM((na, np_, nr, piece, kv), BF16),
            pltpu.VMEM((na, nr, piece, nz * kv), BF16),
            pltpu.VMEM((na, nr, tall, nz * kv), BF16),
            pltpu.VMEM((tall, nz * kv), BF16),
            pltpu.VMEM((chunks, nz * kv, wide), BF16),
            pltpu.VMEM((chunks, tall, wide), F32),
            pltpu.VMEM((chunks, tall, wide), F32),
            pltpu.VMEM((na, tall, cols), F32),
            dma((4,)),
            dma((chunks,)),
            dma((2, 1)),
            dma((2, 2, nx)),
            dma((2, nz)),
            dma((2, np_, nr)),
            dma((2, na, nz)),
            dma((2, na, 2, 2)),
            dma((2, na, 2, nx)),
            dma((2, na, 2, nx)),
            dma((2, 2)),
            dma((2, chunks, 2, far)),
            dma((2, chunks)),
        ],
        compiler_params=pltpu.CompilerParams(
            collective_id=0, has_side_effects=True, vmem_limit_bytes=60 * 1024 * 1024
        ),
    )(col_dosage, col_ancestry, row_dosage, row_ancestry)
    return jnp.transpose(total / spread[:, None, :], (1, 0, 2))


def solution(mesh):
    sizes = (mesh.shape["samp"], mesh.shape["var"], mesh.shape["row"])
    placed = (
        P(None, "var", "samp"),
        P(None, None, "var", "samp"),
        P(None, "var", ("row", "samp")),
        P(None, None, "var", ("row", "samp")),
    )
    return jax.shard_map(
        functools.partial(local, sizes),
        mesh=mesh,
        in_specs=placed,
        out_specs=P(("row", "var"), None, "samp"),
        check_vma=False,
    )
```

time: 301 us -> 86.8 us (0.29)
  waiting for transfers between devices: 214 us -> 0 us
  Pallas kernels: 0 us -> 83.9 us
  blocking collectives: 50.4 us -> 0 us
  between operations: 13.2 us -> 0.01 us
  other arithmetic: 14.4 us -> 2.76 us
  matrix products: 6.43 us -> 0 us
    reduce_scatter x1 -> x0, waiting for transfers between devices: 119 us -> none  [local(): lax.psum_scatter(jnp.einsum('avr,avc->rac', row_centred, col_centred, pre...]
    all_gather x2 -> x0, waiting for transfers between devices: 93.9 us -> none  [the longest x1 71.8 us: local(): lax.all_gather(row_ancestry, 'samp', axis=3, tiled=True)]
    pallas_call x0 -> x1, Pallas kernels: none -> 83.9 us  [local(): pl.pallas_call(functools.partial(kernel, sizes), out_shape=(jax.ShapeDtyp...]
    psum x2 -> x0, blocking collectives: 50.4 us -> none  [the longest x1 36.2 us: local(): counts, sums = lax.psum((local_counts, local_sums), 'samp')]
    reduce_sum x4 -> x0, other arithmetic: 7.43 us -> none  [the longest x2 6.67 us: centre(): jnp.sum(shares * (values[None] - freq[:, None, :, None]), axis=1)]
    dot_general x1 -> x0, matrix products: 6.43 us -> none  [local(): jnp.einsum('avr,avc->rac', row_centred, col_centred, preferred_element_ty...]
    convert_element_type x2 -> x0, other arithmetic: 5.31 us -> none  [centre(): values = dosage.astype(jnp.float32)]
  transfers between devices with their start and end apart: 3 -> 0, of which waited for: 3 -> 0; matrix products, arithmetic and copies ran while one was open for 2% -> 0% of each run, Pallas kernels for 0% -> 0%
where the time goes in v2:
time: 86.8 us; the launch traced here: 86.7 us
  Pallas kernels  83.9 us (97%)
  other arithmetic  2.76 us (3%)
    pallas_call x1, Pallas kernels, local(): pl.pallas_call(functools.partial(kernel, sizes), out_shape=(jax.ShapeDtyp...  83.9 us
    transpose x1, other arithmetic, local(): return jnp.transpose(total / spread[:, None, :], (1, 0, 2))  2.76 us

profile of v2, /device:TPU:1, one launch (start us, length us, event | category | flops | bytes accessed | tf_op | source)
XLA Modules:
  0.0 86.7 jit_solution(11028606529257439700)
XLA Ops:
  0.0 83.9 %shard_map.46 = (f32[3,256,512]{2,1,0:T(8,128)}, f32[3,512]{1,0:T(4,128)}) custom-call(bf16[2,256,512]{2,1,0:T(8,128)(2,1)} %cd_hbm.1, bf16[3,2,256,512]{3,2,1,0:T(8,128)(2,1)} %ca_hbm.1, bf16[2,256,128]{2,1,0:T(8,128)(2,1)} %rd_hbm.1, bf16[3,2,256,128]{3,2,1,0:T(8,128)(2,1)} %ra_hbm.1), custom_call_target="tpu_custom_call" | custom-call | tf_op jit(solution)/shard_map/pallas_call | solution.py:448
  83.9 2.8 %divide_bitcast_fusion = f32[256,3,512]{2,0,1:T(8,128)} fusion(f32[3,256,512]{2,1,0:T(8,128)} %get-tuple-element.7, f32[3,512]{1,0:T(4,128)} %get-tuple-element.8), kind=kLoop, calls=%fused_computation | loop fusion | flops 393216 | bytes 3151872 | tf_op jit(solution)/shard_map/transpose | solution.py:495

commit v3 on v2

--- a/solution.py
+++ b/solution.py
@@ -128,6 +128,13 @@
     for k in (3, 7):
         part[c, k:k + 1, :] = jnp.ones((1, nv), F32)
 
+    loads[2].wait()
+    loads[3].wait()
+    for k in range(2):
+        turned[k] = rd[k].astype(F32).T.astype(BF16)
+        for a in range(na):
+            turned[2 + 2 * a + k] = ra[a, k].astype(F32).T.astype(BF16)
+
     pl.semaphore_wait(barrier, 1 + (nz - 1) + np_ * nr - 1)
 
     sent = []
@@ -147,13 +154,6 @@
 
     push(part.at[c], part.at[c], pair(pair_sem, 0), sibling)
 
-    loads[2].wait()
-    loads[3].wait()
-    for k in range(2):
-        turned[k] = rd[k].astype(F32).T.astype(BF16)
-        for a in range(na):
-            turned[2 + 2 * a + k] = ra[a, k].astype(F32).T.astype(BF16)
-
     arrive(part.at[1 - c], pair(pair_sem, 0))
     stat[p] = part[0] + part[1]
     for i in range(1, nx):
@@ -161,17 +161,24 @@
     for i in range(nx):
         push(stat.at[p], stat.at[p], pair(stat_sem, 1, i), device(chip(((x + i) % nx) * 2 + 1 - h), z, other))
 
-    def t1_piece(i, k):
+    kinds = (pl.ds(0, 4), pl.ds(4, 2 * na - 2))
+
+    def t1_piece(g, i, k):
         rows = pl.ds(aligned(((p + i) % np_) * piece, piece), piece)
         half = pl.ds(aligned((1 - (r + k) % nr) * kv, kv), kv)
-        return turned.at[:, rows, half], raw.at[:, p, r]
-
-    own = pltpu.make_async_copy(*t1_piece(0, 0), t1_sem.at[1, 0, 0])
-    own.start()
-    for i in range(np_):
-        for k in range(nr):
-            if i or k:
-                push(*t1_piece(i, k), pair(t1_sem, i, k), device(chip((p + i) % np_), z, (r + k) % nr))
+        return turned.at[kinds[g], rows, half], raw.at[kinds[g], p, r]
+
+    for g in range(2):
+        pltpu.make_async_copy(*t1_piece(g, 0, 0), t1_sem.at[1, g, 0, 0]).start()
+        for i in range(np_):
+            for k in range(nr):
+                if i or k:
+                    push(*t1_piece(g, i, k), pair(t1_sem, g, i, k), device(chip((p + i) % np_), z, (r + k) % nr))
+
+    def t1_wait(g):
+        for i in range(np_):
+            for k in range(nr):
+                arrive(raw.at[kinds[g], (p + np_ - i) % np_, (r + nr - k) % nr], pair(t1_sem, g, i, k))
 
     for i in range(1, nx):
         arrive(stat.at[((x + nx - i) % nx) * 2 + h], pair(stat_sem, 0, i))
@@ -185,10 +192,6 @@
     for a in range(na):
         freq[a] = jnp.broadcast_to(ratio[a:a + 1, :], (128, nv)).T
 
-    for i in range(np_):
-        for k in range(nr):
-            arrive(raw.at[:, (p + np_ - i) % np_, (r + nr - k) % nr], pair(t1_sem, i, k))
-
     def centre_rows(a):
         f = ratios[a:a + 1, pl.ds(aligned(other * kv, kv), kv)]
         f = jnp.broadcast_to(f, (piece, kv))[None, None]
@@ -320,87 +323,95 @@
         o_buf[a, :, out_lanes(j)] += c_recv[j]
         store(j)
 
+    def share_spread():
+        spreads[z, 0:4, :] = jnp.broadcast_to(jnp.sum(ratio * (1.0 - ratio), axis=1, keepdims=True), (4, 128))
+        spreads[z, 4:8, :] = jnp.zeros((4, 128), F32)
+        for i in range(1, nz):
+            push(spreads.at[z], spreads.at[z], pair(spread_sem, i), device(s, (z + i) % nz, r))
+
+    centre_cols(0)
+    launch(0)
+    t1_wait(0)
     centre_rows(0)
     t2_send(0)
-    for j in range(2):
+    for j in range(1, 3):
         centre_cols(j)
         launch(j)
-    centre_cols(2)
-    launch(2)
+    t1_wait(1)
     for a in range(1, na):
         centre_rows(a)
         t2_send(a)
-    spreads[z, 0:4, :] = jnp.broadcast_to(jnp.sum(ratio * (1.0 - ratio), axis=1, keepdims=True), (4, 128))
-    spreads[z, 4:8, :] = jnp.zeros((4, 128), F32)
-    for i in range(1, nz):
-        push(spreads.at[z], spreads.at[z], pair(spread_sem, i), device(s, (z + i) % nz, r))
+    share_spread()
     for j in range(3, len(chunks)):
         centre_cols(j)
-
     hop(0, 1)
     t2_wait(0)
     g1_send(0, 0)
-    g1_send(0, 1)
     hop(1, 1)
     hop(2, 1)
     for a in range(1, na):
         t2_wait(a)
         g1_send(a, 0)
+    g1_wait(0, 0)
+    g2_send(0, 0)
+    for a in range(na):
         g1_send(a, 1)
     hop(0, 2)
     hop(1, 2)
-    g1_wait(0, 0)
-    g2_send(0, 0)
-    g1_wait(0, 1)
-    g2_send(0, 1)
     hop(2, 2)
-    for a in range(1, na):
-        for o in range(2):
-            g1_wait(a, o)
-            g2_send(a, o)
+    g1_wait(1, 0)
+    g2_send(1, 0)
     hop(0, 3)
     launch(3)
     hop(1, 3)
+    hop(2, 3)
     launch(4)
-    hop(2, 3)
-    launch(5)
     g2_wait(0, 0)
+    g1_wait(2, 0)
+    g2_send(2, 0)
     f_wait(0, 0)
     hop(0, 4)
     hand_over(0)
-    launch(6)
+    launch(5)
     hop(1, 4)
     hand_over(1)
-    g2_wait(1, 0)
+    launch(6)
+    g1_wait(0, 1)
+    g2_send(0, 1)
     hop(3, 1)
     hop(2, 4)
+    g2_wait(1, 0)
     f_wait(1, 0)
     hand_over(2)
     hop(4, 1)
+    g1_wait(1, 1)
+    g2_send(1, 1)
     hop(5, 1)
     hop(6, 1)
+    g2_wait(2, 0)
+    far_send()
+    g1_wait(2, 1)
+    g2_send(2, 1)
+    hop(3, 2)
+    hop(4, 2)
     g2_wait(0, 1)
+    hop(5, 2)
     f_wait(0, 1)
     keep(0)
     keep(1)
-    hop(3, 2)
+    hop(6, 2)
     g2_wait(1, 1)
-    g2_wait(2, 0)
+    finish(0)
     f_wait(1, 1)
     keep(2)
-    hop(4, 2)
-    hop(5, 2)
-    g2_wait(2, 1)
-    f_wait(2, 0)
-    f_wait(2, 1)
-    far_send()
-    hop(6, 2)
-    finish(0)
     hop(3, 3)
     hop(4, 3)
+    g2_wait(2, 1)
     hop(5, 3)
     far_wait()
     hop(6, 3)
+    f_wait(2, 0)
+    f_wait(2, 1)
     finish(1)
     hop(3, 4)
     hand_over(3)
@@ -479,7 +490,7 @@
             dma((2, 1)),
             dma((2, 2, nx)),
             dma((2, nz)),
-            dma((2, np_, nr)),
+            dma((2, 2, np_, nr)),
             dma((2, na, nz)),
             dma((2, na, 2, 2)),
             dma((2, na, 2, nx)),

time: 86.8 us -> 78 us (0.90); the launches traced: 86.7 us -> 76.8 us
  Pallas kernels: 83.9 us -> 74.1 us
    pallas_call x1, Pallas kernels: 83.9 us -> 74.1 us  [local(): pl.pallas_call(functools.partial(kernel, sizes), out_shape=(jax.ShapeDtyp...]
where the time goes in v3:
time: 78 us; the launch traced here: 76.8 us
  Pallas kernels  74.1 us (95%)
  other arithmetic  2.76 us (4%)
    pallas_call x1, Pallas kernels, local(): pl.pallas_call(functools.partial(kernel, sizes), out_shape=(jax.ShapeDtyp...  74.1 us
    transpose x1, other arithmetic, local(): return jnp.transpose(total / spread[:, None, :], (1, 0, 2))  2.76 us

profile of v3, /device:TPU:1, one launch (start us, length us, event | category | flops | bytes accessed | tf_op | source)
XLA Modules:
  0.0 76.8 jit_solution(9494464814930139294)
XLA Ops:
  0.0 74.1 %shard_map.46 = (f32[3,256,512]{2,1,0:T(8,128)}, f32[3,512]{1,0:T(4,128)}) custom-call(bf16[2,256,512]{2,1,0:T(8,128)(2,1)} %cd_hbm.1, bf16[3,2,256,512]{3,2,1,0:T(8,128)(2,1)} %ca_hbm.1, bf16[2,256,128]{2,1,0:T(8,128)(2,1)} %rd_hbm.1, bf16[3,2,256,128]{3,2,1,0:T(8,128)(2,1)} %ra_hbm.1), custom_call_target="tpu_custom_call" | custom-call | tf_op jit(solution)/shard_map/pallas_call | solution.py:459
  74.1 2.8 %divide_bitcast_fusion = f32[256,3,512]{2,0,1:T(8,128)} fusion(f32[3,256,512]{2,1,0:T(8,128)} %get-tuple-element.7, f32[3,512]{1,0:T(4,128)} %get-tuple-element.8), kind=kLoop, calls=%fused_computation | loop fusion | flops 393216 | bytes 3151872 | tf_op jit(solution)/shard_map/transpose | solution.py:506

commit v4 on v3

--- a/solution.py
+++ b/solution.py
@@ -10,7 +10,8 @@
 MESH = pl.DeviceIdType.MESH
 F32 = jnp.float32
 BF16 = jnp.bfloat16
-HALVES = 2
+PARTS = 4
+WHOLE = 3
 STEP = 32
 
 
@@ -73,7 +74,7 @@
     na = ca.shape[0]
     nv, cols = cd.shape[1:]
     kv = nv // nr
-    wide = cols // HALVES
+    wide = cols // PARTS
     piece = rd.shape[2] // np_
     far = nz // 2
     sibling = device(s + 1 - 2 * c, z, r)
@@ -170,15 +171,14 @@
 
     for g in range(2):
         pltpu.make_async_copy(*t1_piece(g, 0, 0), t1_sem.at[1, g, 0, 0]).start()
-        for i in range(np_):
-            for k in range(nr):
+        for k in range(nr):
+            for i in range(np_):
                 if i or k:
                     push(*t1_piece(g, i, k), pair(t1_sem, g, i, k), device(chip((p + i) % np_), z, (r + k) % nr))
 
-    def t1_wait(g):
+    def t1_wait(g, k):
         for i in range(np_):
-            for k in range(nr):
-                arrive(raw.at[kinds[g], (p + np_ - i) % np_, (r + nr - k) % nr], pair(t1_sem, g, i, k))
+            arrive(raw.at[kinds[g], (p + np_ - i) % np_, (r + nr - k) % nr], pair(t1_sem, g, i, k))
 
     for i in range(1, nx):
         arrive(stat.at[((x + nx - i) % nx) * 2 + h], pair(stat_sem, 0, i))
@@ -192,33 +192,34 @@
     for a in range(na):
         freq[a] = jnp.broadcast_to(ratio[a:a + 1, :], (128, nv)).T
 
-    def centre_rows(a):
+    def centre_rows(a, o):
+        ry = r if o == 0 else other
         f = ratios[a:a + 1, pl.ds(aligned(other * kv, kv), kv)]
-        f = jnp.broadcast_to(f, (piece, kv))[None, None]
-        value = raw[2 + 2 * a].astype(F32) * (raw[0].astype(F32) - f)
-        value = value + raw[3 + 2 * a].astype(F32) * (raw[1].astype(F32) - f)
-        centred[a] = value.astype(BF16)
-        hold[a, :, :, pl.ds(aligned(z * kv, kv), kv)] = centred[a, z]
-
-    def hold_from(a, zz):
-        return hold.at[a, :, :, pl.ds(aligned(zz * kv, kv), kv)]
-
-    def t2_send(a):
+        f = jnp.broadcast_to(f, (piece, kv))[None]
+        value = raw[2 + 2 * a, :, ry].astype(F32) * (raw[0, :, ry].astype(F32) - f)
+        value = value + raw[3 + 2 * a, :, ry].astype(F32) * (raw[1, :, ry].astype(F32) - f)
+        centred[a, o] = value.astype(BF16)
+        hold[a, o, :, pl.ds(aligned(z * kv, kv), kv)] = centred[a, o, z]
+
+    def hold_from(a, o, zz):
+        return hold.at[a, o, :, pl.ds(aligned(zz * kv, kv), kv)]
+
+    def t2_send(a, o):
         for i in range(1, nz):
             to = (z + i) % nz
-            push(centred.at[a, to], hold_from(a, z), pair(t2_sem, a, i), device(s, to, r))
+            push(centred.at[a, o, to], hold_from(a, o, z), pair(t2_sem, a, o, i), device(s, to, r))
 
     def a_rows(a, ry, core, first, count):
         return a_buf.at[a, ry, pl.ds(aligned(core * 128 + first * piece, piece), count * piece), :]
 
-    def t2_wait(a):
+    def t2_wait(a, o):
         for i in range(1, nz):
-            arrive(hold_from(a, (z + nz - i) % nz), pair(t2_sem, a, i))
+            arrive(hold_from(a, o, (z + nz - i) % nz), pair(t2_sem, a, o, i))
 
     def g1_send(a, o):
         ry = r if o == 0 else other
         for k, who in enumerate((mate, across)):
-            push(hold.at[a, ry], a_rows(a, ry, c, p, 1), pair(g1_sem, a, o, k), who)
+            push(hold.at[a, o], a_rows(a, ry, c, p, 1), pair(g1_sem, a, o, k), who)
 
     def g1_wait(a, o):
         ry = other if o == 0 else r
@@ -255,10 +256,8 @@
         push(a_far.at[far_rows(c)], a_far.at[far_rows(c)], pair(far_sem, 1), sibling)
         arrive(a_far.at[far_rows(1 - c)], pair(far_sem, 1))
 
-    chunks = [(a, half, False) for a in range(na) for half in range(HALVES)]
-    both = [(na - 1, HALVES - 1)]
-    chunks += [(a, half, True) for a, half in both]
-    handed = [j for j, (a, half, extra) in enumerate(chunks) if (a, half) not in both]
+    chunks = [(a, half, False) for a in range(na) for half in range(PARTS)]
+    chunks += [(na - 1, PARTS - 1 - i, True) for i in range(WHOLE)]
 
     def centre_cols(j):
         a, half, extra = chunks[j]
@@ -311,6 +310,12 @@
 
     stores = []
 
+    def both(j, extra):
+        a = chunks[j][0]
+        value = jnp.dot(a_buf[a, r], b_buf[j], preferred_element_type=F32)
+        o_buf[a, :, out_lanes(j)] = value + jnp.dot(a_far[...], b_buf[extra], preferred_element_type=F32)
+        store(j)
+
     def store(j):
         a = chunks[j][0]
         copy = pltpu.make_async_copy(o_buf.at[a, :, out_lanes(j)], out_ref.at[a, :, out_lanes(j)], out_sem.at[j])
@@ -331,101 +336,179 @@
 
     centre_cols(0)
     launch(0)
-    t1_wait(0)
-    centre_rows(0)
-    t2_send(0)
-    for j in range(1, 3):
-        centre_cols(j)
-        launch(j)
-    t1_wait(1)
-    for a in range(1, na):
-        centre_rows(a)
-        t2_send(a)
+    centre_cols(1)
+    launch(1)
+    centre_cols(2)
+    launch(2)
     share_spread()
-    for j in range(3, len(chunks)):
-        centre_cols(j)
+    t1_wait(0, 0)
+    centre_rows(0, 0)
+    t2_send(0, 0)
+    centre_cols(3)
+    launch(3)
+    t1_wait(1, 0)
+    centre_rows(1, 0)
+    t2_send(1, 0)
     hop(0, 1)
-    t2_wait(0)
+    centre_rows(2, 0)
+    t2_send(2, 0)
+    hop(1, 1)
+    t1_wait(0, 1)
+    centre_rows(0, 1)
+    t2_send(0, 1)
+    hop(2, 1)
+    t1_wait(1, 1)
+    centre_rows(1, 1)
+    t2_send(1, 1)
+    centre_rows(2, 1)
+    t2_send(2, 1)
+    hop(3, 1)
+    hop(0, 2)
+    t2_wait(0, 0)
     g1_send(0, 0)
-    hop(1, 1)
-    hop(2, 1)
-    for a in range(1, na):
-        t2_wait(a)
-        g1_send(a, 0)
+    hop(1, 2)
+    t2_wait(1, 0)
+    g1_send(1, 0)
+    hop(2, 2)
+    t2_wait(2, 0)
+    g1_send(2, 0)
     g1_wait(0, 0)
     g2_send(0, 0)
-    for a in range(na):
-        g1_send(a, 1)
-    hop(0, 2)
-    hop(1, 2)
-    hop(2, 2)
+    centre_cols(4)
+    launch(4)
+    t2_wait(0, 1)
+    g1_send(0, 1)
+    centre_cols(5)
+    launch(5)
+    hop(3, 2)
     g1_wait(1, 0)
     g2_send(1, 0)
     hop(0, 3)
-    launch(3)
+    t2_wait(1, 1)
+    g1_send(1, 1)
+    centre_cols(6)
+    launch(6)
+    g1_wait(2, 0)
+    g2_send(2, 0)
     hop(1, 3)
     hop(2, 3)
-    launch(4)
-    g2_wait(0, 0)
-    g1_wait(2, 0)
-    g2_send(2, 0)
-    f_wait(0, 0)
-    hop(0, 4)
-    hand_over(0)
-    launch(5)
-    hop(1, 4)
-    hand_over(1)
-    launch(6)
+    t2_wait(2, 1)
+    g1_send(2, 1)
+    centre_cols(7)
+    launch(7)
+    hop(4, 1)
     g1_wait(0, 1)
     g2_send(0, 1)
-    hop(3, 1)
-    hop(2, 4)
-    g2_wait(1, 0)
-    f_wait(1, 0)
-    hand_over(2)
-    hop(4, 1)
+    hop(5, 1)
+    hop(3, 3)
     g1_wait(1, 1)
     g2_send(1, 1)
-    hop(5, 1)
+    hop(0, 4)
+    g2_wait(0, 0)
+    centre_cols(8)
+    launch(8)
+    hop(1, 4)
     hop(6, 1)
+    hop(2, 4)
+    g1_wait(2, 1)
+    g2_send(2, 1)
+    centre_cols(11)
+    launch(11)
+    f_wait(0, 0)
+    hand_over(0)
+    hand_over(1)
+    hand_over(2)
+    hop(4, 2)
+    g2_wait(1, 0)
+    hop(5, 2)
+    hop(3, 4)
+    hand_over(3)
+    centre_cols(12)
+    launch(12)
+    hop(7, 1)
+    hop(8, 1)
+    f_wait(1, 0)
+    hop(6, 2)
+    hop(11, 1)
     g2_wait(2, 0)
     far_send()
-    g1_wait(2, 1)
-    g2_send(2, 1)
-    hop(3, 2)
-    hop(4, 2)
+    hop(4, 3)
+    hop(5, 3)
+    f_wait(2, 0)
+    hop(12, 1)
+    hop(7, 2)
     g2_wait(0, 1)
-    hop(5, 2)
+    hop(8, 2)
+    hop(6, 3)
     f_wait(0, 1)
     keep(0)
-    keep(1)
-    hop(6, 2)
-    g2_wait(1, 1)
-    finish(0)
-    f_wait(1, 1)
-    keep(2)
-    hop(3, 3)
-    hop(4, 3)
-    g2_wait(2, 1)
-    hop(5, 3)
-    far_wait()
-    hop(6, 3)
-    f_wait(2, 0)
-    f_wait(2, 1)
-    finish(1)
-    hop(3, 4)
-    hand_over(3)
-    keep(3)
+    centre_cols(10)
+    launch(10)
+    hop(11, 2)
     hop(4, 4)
     hand_over(4)
+    hop(5, 4)
+    hand_over(5)
+    centre_cols(13)
+    launch(13)
+    g2_wait(1, 1)
+    centre_cols(9)
+    launch(9)
+    hop(7, 3)
+    hop(12, 2)
+    keep(1)
+    hop(8, 3)
+    hop(6, 4)
+    hand_over(6)
+    f_wait(1, 1)
+    g2_wait(2, 1)
+    hop(10, 1)
+    far_wait()
+    keep(2)
+    hop(11, 3)
+    keep(3)
     keep(4)
+    centre_cols(14)
+    launch(14)
+    f_wait(2, 1)
+    hop(13, 1)
+    keep(5)
+    hop(9, 1)
+    keep(6)
+    hop(7, 4)
+    hand_over(7)
+    keep(7)
+    hop(12, 3)
+    hop(8, 4)
+    hand_over(8)
+    keep(8)
+    hop(10, 2)
+    finish(0)
+    hop(11, 4)
+    finish(1)
     finish(2)
-    hop(5, 4)
-    hop(6, 4)
-    a, lanes = chunks[5][0], out_lanes(5)
-    o_buf[a, :, lanes] = jnp.dot(a_buf[a, r], b_buf[5], preferred_element_type=F32)
-    o_buf[a, :, lanes] += jnp.dot(a_far[...], b_buf[6], preferred_element_type=F32)
-    store(5)
+    finish(3)
+    finish(4)
+    hop(14, 1)
+    hop(13, 2)
+    hop(9, 2)
+    hop(12, 4)
+    both(11, 12)
+    finish(5)
+    hop(10, 3)
+    hop(14, 2)
+    hop(13, 3)
+    finish(6)
+    hop(9, 3)
+    hop(10, 4)
+    hop(14, 3)
+    hop(13, 4)
+    both(10, 13)
+    finish(7)
+    hop(9, 4)
+    hop(14, 4)
+    both(9, 14)
+    finish(8)
 
     for i in range(1, nz):
         arrive(spreads.at[(z + nz - i) % nz], pair(spread_sem, i))
@@ -434,9 +517,6 @@
         spread = spread + spreads[i]
     for a in range(na):
         spread_ref[a:a + 1, :] = jnp.concatenate([spread[a:a + 1, :]] * (cols // 128), axis=1)
-    for j in handed[3:]:
-        finish(j)
-
     for copy in sent:
         copy.wait_send()
     for copy in stores:
@@ -451,9 +531,9 @@
     rows = row_dosage.shape[2]
     kv = nv // nr
     tall = 2 * rows
-    wide = cols // HALVES
+    wide = cols // PARTS
     piece = rows // np_
-    chunks = na * HALVES + 1
+    chunks = na * PARTS + WHOLE
     far = nz // 2
     dma = pltpu.SemaphoreType.DMA
     total, spread = pl.pallas_call(
@@ -477,7 +557,7 @@
             pltpu.VMEM((nz, 8, 128), F32),
             pltpu.VMEM((2 + 2 * na, rows, nv), BF16),
             pltpu.VMEM((2 + 2 * na, np_, nr, piece, kv), BF16),
-            pltpu.VMEM((na, np_, nr, piece, kv), BF16),
+            pltpu.VMEM((na, nr, np_, piece, kv), BF16),
             pltpu.VMEM((na, nr, piece, nz * kv), BF16),
             pltpu.VMEM((na, nr, tall, nz * kv), BF16),
             pltpu.VMEM((tall, nz * kv), BF16),
@@ -491,7 +571,7 @@
             dma((2, 2, nx)),
             dma((2, nz)),
             dma((2, 2, np_, nr)),
-            dma((2, na, nz)),
+            dma((2, na, 2, nz)),
             dma((2, na, 2, 2)),
             dma((2, na, 2, nx)),
             dma((2, na, 2, nx)),

time: 78 us -> 72.4 us (0.928)
  Pallas kernels: 74.1 us -> 69.2 us
    pallas_call x1, Pallas kernels: 74.1 us -> 69.2 us  [local(): pl.pallas_call(functools.partial(kernel, sizes), out_shape=(jax.ShapeDtyp...]
where the time goes in v4:
time: 72.4 us; the launch traced here: 72 us
  Pallas kernels  69.2 us (96%)
  other arithmetic  2.76 us (4%)
    pallas_call x1, Pallas kernels, local(): pl.pallas_call(functools.partial(kernel, sizes), out_shape=(jax.ShapeDtyp...  69.2 us
    transpose x1, other arithmetic, local(): return jnp.transpose(total / spread[:, None, :], (1, 0, 2))  2.76 us

profile of v4, /device:TPU:1, one launch (start us, length us, event | category | flops | bytes accessed | tf_op | source)
XLA Modules:
  0.0 72.0 jit_solution(7313525211271333183)
XLA Ops:
  0.0 69.2 %shard_map.46 = (f32[3,256,512]{2,1,0:T(8,128)}, f32[3,512]{1,0:T(4,128)}) custom-call(bf16[2,256,512]{2,1,0:T(8,128)(2,1)} %cd_hbm.1, bf16[3,2,256,512]{3,2,1,0:T(8,128)(2,1)} %ca_hbm.1, bf16[2,256,128]{2,1,0:T(8,128)(2,1)} %rd_hbm.1, bf16[3,2,256,128]{3,2,1,0:T(8,128)(2,1)} %ra_hbm.1), custom_call_target="tpu_custom_call" | custom-call | tf_op jit(solution)/shard_map/pallas_call | solution.py:539
  69.2 2.8 %divide_bitcast_fusion = f32[256,3,512]{2,0,1:T(8,128)} fusion(f32[3,256,512]{2,1,0:T(8,128)} %get-tuple-element.7, f32[3,512]{1,0:T(4,128)} %get-tuple-element.8), kind=kLoop, calls=%fused_computation | loop fusion | flops 393216 | bytes 3151872 | tf_op jit(solution)/shard_map/transpose | solution.py:586

commit v5 on v4

--- a/solution.py
+++ b/solution.py
@@ -29,7 +29,7 @@
     ca_hbm,
     rd_hbm,
     ra_hbm,
-    out_ref,
+    o_buf,
     spread_ref,
     cd,
     ca,
@@ -50,9 +50,7 @@
     b_buf,
     c_send,
     c_recv,
-    o_buf,
     in_sem,
-    out_sem,
     pair_sem,
     stat_sem,
     spread_sem,
@@ -308,25 +306,15 @@
         a = chunks[j][0]
         o_buf[a, :, out_lanes(j)] = jnp.dot(a_buf[a, r], b_buf[j], preferred_element_type=F32)
 
-    stores = []
-
     def both(j, extra):
         a = chunks[j][0]
         value = jnp.dot(a_buf[a, r], b_buf[j], preferred_element_type=F32)
         o_buf[a, :, out_lanes(j)] = value + jnp.dot(a_far[...], b_buf[extra], preferred_element_type=F32)
-        store(j)
-
-    def store(j):
-        a = chunks[j][0]
-        copy = pltpu.make_async_copy(o_buf.at[a, :, out_lanes(j)], out_ref.at[a, :, out_lanes(j)], out_sem.at[j])
-        copy.start()
-        stores.append(copy)
 
     def finish(j):
         a = chunks[j][0]
         arrive(c_recv.at[j], pair(c_sem, j))
         o_buf[a, :, out_lanes(j)] += c_recv[j]
-        store(j)
 
     def share_spread():
         spreads[z, 0:4, :] = jnp.broadcast_to(jnp.sum(ratio * (1.0 - ratio), axis=1, keepdims=True), (4, 128))
@@ -519,8 +507,6 @@
         spread_ref[a:a + 1, :] = jnp.concatenate([spread[a:a + 1, :]] * (cols // 128), axis=1)
     for copy in sent:
         copy.wait_send()
-    for copy in stores:
-        copy.wait()
 
 
 def local(sizes, col_dosage, col_ancestry, row_dosage, row_ancestry):
@@ -536,14 +522,16 @@
     chunks = na * PARTS + WHOLE
     far = nz // 2
     dma = pltpu.SemaphoreType.DMA
+    args = (col_dosage, col_ancestry, row_dosage, row_ancestry)
+    args = [pltpu.with_memory_space_constraint(v, pltpu.HBM) for v in args]
     total, spread = pl.pallas_call(
         functools.partial(kernel, sizes),
         out_shape=(
-            jax.ShapeDtypeStruct((na, tall, cols), F32),
+            pltpu.VMEM((na, tall, cols), F32),
             jax.ShapeDtypeStruct((na, cols), F32),
         ),
         in_specs=[pl.BlockSpec(memory_space=pltpu.HBM)] * 4,
-        out_specs=(pl.BlockSpec(memory_space=pl.ANY), pl.BlockSpec(memory_space=pltpu.VMEM)),
+        out_specs=(pl.BlockSpec(memory_space=pltpu.VMEM), pl.BlockSpec(memory_space=pltpu.VMEM)),
         scratch_shapes=[
             pltpu.VMEM(col_dosage.shape, BF16),
             pltpu.VMEM(col_ancestry.shape, BF16),
@@ -564,9 +552,7 @@
             pltpu.VMEM((chunks, nz * kv, wide), BF16),
             pltpu.VMEM((chunks, tall, wide), F32),
             pltpu.VMEM((chunks, tall, wide), F32),
-            pltpu.VMEM((na, tall, cols), F32),
             dma((4,)),
-            dma((chunks,)),
             dma((2, 1)),
             dma((2, 2, nx)),
             dma((2, nz)),
@@ -580,9 +566,9 @@
             dma((2, chunks)),
         ],
         compiler_params=pltpu.CompilerParams(
-            collective_id=0, has_side_effects=True, vmem_limit_bytes=60 * 1024 * 1024
+            collective_id=0, has_side_effects=True, vmem_limit_bytes=44 * 1024 * 1024
         ),
-    )(col_dosage, col_ancestry, row_dosage, row_ancestry)
+    )(*args)
     return jnp.transpose(total / spread[:, None, :], (1, 0, 2))
 
 

time: 72.4 us -> 69.9 us (0.965)
  other arithmetic: 2.76 us -> 1.4 us
  Pallas kernels: 69.2 us -> 68.2 us
    transpose x1, other arithmetic: 2.76 us -> 1.4 us  [local(): return jnp.transpose(total / spread[:, None, :], (1, 0, 2))]
    pallas_call x1, Pallas kernels: 69.2 us -> 68.2 us  [local(): pl.pallas_call(functools.partial(kernel, sizes), out_shape=(pltpu.VMEM((n...]
where the time goes in v5:
time: 69.9 us; the launch traced here: 69.6 us
  Pallas kernels  68.2 us (98%)
  other arithmetic  1.4 us (2%)
    pallas_call x1, Pallas kernels, local(): pl.pallas_call(functools.partial(kernel, sizes), out_shape=(pltpu.VMEM((n...  68.2 us
    transpose x1, other arithmetic, local(): return jnp.transpose(total / spread[:, None, :], (1, 0, 2))  1.4 us

profile of v5, /device:TPU:1, one launch (start us, length us, event | category | flops | bytes accessed | tf_op | source)
XLA Modules:
  0.0 69.6 jit_solution(5533637176958264626)
XLA Ops:
  0.0 68.2 %shard_map.46 = (f32[3,256,512]{2,1,0:T(8,128)S(1)}, f32[3,512]{1,0:T(4,128)S(1)}) custom-call(bf16[2,256,512]{2,1,0:T(8,128)(2,1)} %cd_hbm.1, bf16[3,2,256,512]{3,2,1,0:T(8,128)(2,1)} %ca_hbm.1, bf16[2,256,128]{2,1,0:T(8,128)(2,1)} %rd_hbm.1, bf16[3,2,256,128]{3,2,1,0:T(8,128)(2,1)} %ra_hbm.1), custom_call_target="tpu_custom_call" | custom-call | tf_op jit(solution)/shard_map/pallas_call | solution.py:527
  68.2 1.4 %divide_bitcast_fusion = f32[256,3,512]{2,0,1:T(8,128)} fusion(f32[3,256,512]{2,1,0:T(8,128)S(1)} %get-tuple-element.7, f32[3,512]{1,0:T(4,128)S(1)} %get-tuple-element.8), kind=kLoop, calls=%fused_computation | loop fusion | flops 393216 | bytes 3151872 | tf_op jit(solution)/shard_map/transpose | solution.py:572

commit v6 on v5

--- a/solution.py
+++ b/solution.py
@@ -11,7 +11,7 @@
 F32 = jnp.float32
 BF16 = jnp.bfloat16
 PARTS = 4
-WHOLE = 3
+WHOLE = 2
 STEP = 32
 
 
@@ -59,7 +59,7 @@
     g1_sem,
     g2_sem,
     f_sem,
-    far_sem,
+    s_sem,
     b_sem,
     c_sem,
 ):
@@ -207,55 +207,51 @@
             to = (z + i) % nz
             push(centred.at[a, o, to], hold_from(a, o, z), pair(t2_sem, a, o, i), device(s, to, r))
 
-    def a_rows(a, ry, core, first, count):
-        return a_buf.at[a, ry, pl.ds(aligned(core * 128 + first * piece, piece), count * piece), :]
+    def a_rows(a, o, core, first, count):
+        rows = pl.ds(aligned(core * 128 + first * piece, piece), count * piece)
+        if (a, o) == (na - 1, 0):
+            return a_far.at[rows, :]
+        return a_buf.at[a, other if o == 0 else r, rows, :]
 
     def t2_wait(a, o):
         for i in range(1, nz):
             arrive(hold_from(a, o, (z + nz - i) % nz), pair(t2_sem, a, o, i))
 
     def g1_send(a, o):
-        ry = r if o == 0 else other
+        if (a, o) == (na - 1, 0):
+            a_far[pl.ds(aligned(c * 128 + p * piece, piece), piece), :] = hold[a, o]
+            push(hold.at[a, o], a_rows(a, o, c, p, 1), pair(g1_sem, a, o, 1), device(chip(x * 2 + 1 - h), z, r))
+            return
+        rows = pl.ds(aligned(c * 128 + p * piece, piece), piece)
+        dst = a_buf.at[a, r if o == 0 else other, rows, :]
         for k, who in enumerate((mate, across)):
-            push(hold.at[a, o], a_rows(a, ry, c, p, 1), pair(g1_sem, a, o, k), who)
+            push(hold.at[a, o], dst, pair(g1_sem, a, o, k), who)
 
     def g1_wait(a, o):
-        ry = other if o == 0 else r
-        arrive(a_rows(a, ry, c, p, 1), pair(g1_sem, a, o, 0))
-        arrive(a_rows(a, ry, c, x * 2 + 1 - h, 1), pair(g1_sem, a, o, 1))
+        if (a, o) != (na - 1, 0):
+            arrive(a_rows(a, o, c, p, 1), pair(g1_sem, a, o, 0))
+        arrive(a_rows(a, o, c, x * 2 + 1 - h, 1), pair(g1_sem, a, o, 1))
 
     def g2_send(a, o):
-        ry = other if o == 0 else r
-        ref = a_rows(a, ry, c, x * 2, 2)
+        ref = a_rows(a, o, c, x * 2, 2)
         for i in range(1, nx):
             push(ref, ref, pair(g2_sem, a, o, i), device(chip(((x + i) % nx) * 2 + h), z, r))
         push(ref, ref, pair(f_sem, a, o, 0), sibling)
 
     def g2_wait(a, o):
-        ry = other if o == 0 else r
         for i in range(1, nx):
-            ref = a_rows(a, ry, c, ((x + nx - i) % nx) * 2, 2)
+            ref = a_rows(a, o, c, ((x + nx - i) % nx) * 2, 2)
             arrive(ref, pair(g2_sem, a, o, i))
             push(ref, ref, pair(f_sem, a, o, i), sibling)
 
     def f_wait(a, o):
-        ry = other if o == 0 else r
         for i in range(nx):
-            arrive(a_rows(a, ry, 1 - c, ((x + nx - i) % nx) * 2, 2), pair(f_sem, a, o, i))
-
-    def far_rows(core):
-        return pl.ds(aligned(core * 128, 128), 128)
-
-    def far_send():
-        push(a_buf.at[na - 1, other, far_rows(c)], a_far.at[far_rows(c)], pair(far_sem, 0), across)
-
-    def far_wait():
-        arrive(a_far.at[far_rows(c)], pair(far_sem, 0))
-        push(a_far.at[far_rows(c)], a_far.at[far_rows(c)], pair(far_sem, 1), sibling)
-        arrive(a_far.at[far_rows(1 - c)], pair(far_sem, 1))
+            arrive(a_rows(a, o, 1 - c, ((x + nx - i) % nx) * 2, 2), pair(f_sem, a, o, i))
 
     chunks = [(a, half, False) for a in range(na) for half in range(PARTS)]
-    chunks += [(na - 1, PARTS - 1 - i, True) for i in range(WHOLE)]
+    last = [(na - 1) * PARTS + i for i in range(PARTS)]
+    shared = last[:PARTS - WHOLE]
+    chunks += [(na - 1, i, True) for i in range(PARTS)]
 
     def centre_cols(j):
         a, half, extra = chunks[j]
@@ -290,9 +286,18 @@
 
     def hop(j, d):
         for way in range(2):
-            arrive(b_part(j, (z + (nz - ways[way]) * d) % nz, way, d), pair(b_sem, j, way, d - 1))
+            zz = (z + (nz - ways[way]) * d) % nz
+            arrive(b_part(j, zz, way, d), pair(b_sem, j, way, d - 1))
             if d < far:
                 b_move(j, way, d + 1)
+            if j in shared:
+                push(b_part(j, zz, way, d), b_part(j + PARTS, zz, way, d), pair(s_sem, j - last[0], way, d - 1), mate)
+
+    def share_wait(j):
+        for d in range(1, far + 1):
+            for way in range(2):
+                zz = (z + (nz - ways[way]) * d) % nz
+                arrive(b_part(j + PARTS, zz, way, d), pair(s_sem, j - last[0], way, d - 1))
 
     def hand_over(j):
         a = chunks[j][0]
@@ -308,6 +313,8 @@
 
     def both(j, extra):
         a = chunks[j][0]
+        if j in shared:
+            share_wait(j)
         value = jnp.dot(a_buf[a, r], b_buf[j], preferred_element_type=F32)
         o_buf[a, :, out_lanes(j)] = value + jnp.dot(a_far[...], b_buf[extra], preferred_element_type=F32)
 
@@ -326,177 +333,169 @@
     launch(0)
     centre_cols(1)
     launch(1)
-    centre_cols(2)
-    launch(2)
+    centre_cols(8)
+    launch(8)
     share_spread()
+    centre_cols(12)
+    centre_cols(13)
+    centre_cols(9)
+    launch(9)
     t1_wait(0, 0)
     centre_rows(0, 0)
     t2_send(0, 0)
-    centre_cols(3)
-    launch(3)
+    hop(0, 1)
     t1_wait(1, 0)
     centre_rows(1, 0)
     t2_send(1, 0)
-    hop(0, 1)
     centre_rows(2, 0)
     t2_send(2, 0)
     hop(1, 1)
+    hop(8, 1)
     t1_wait(0, 1)
     centre_rows(0, 1)
     t2_send(0, 1)
-    hop(2, 1)
+    hop(9, 1)
     t1_wait(1, 1)
+    centre_rows(2, 1)
+    t2_send(2, 1)
     centre_rows(1, 1)
     t2_send(1, 1)
-    centre_rows(2, 1)
-    t2_send(2, 1)
-    hop(3, 1)
     hop(0, 2)
+    hop(1, 2)
     t2_wait(0, 0)
     g1_send(0, 0)
-    hop(1, 2)
+    hop(8, 2)
     t2_wait(1, 0)
     g1_send(1, 0)
-    hop(2, 2)
+    hop(9, 2)
     t2_wait(2, 0)
     g1_send(2, 0)
+    centre_cols(2)
+    launch(2)
+    centre_cols(3)
+    launch(3)
     g1_wait(0, 0)
     g2_send(0, 0)
+    hop(0, 3)
+    hop(1, 3)
+    t2_wait(0, 1)
+    g1_send(0, 1)
     centre_cols(4)
     launch(4)
-    t2_wait(0, 1)
-    g1_send(0, 1)
+    hop(8, 3)
+    hop(9, 3)
+    g1_wait(1, 0)
+    g2_send(1, 0)
+    hop(2, 1)
+    t2_wait(1, 1)
+    g1_send(1, 1)
+    hop(3, 1)
+    hop(0, 4)
+    hop(1, 4)
+    t2_wait(2, 1)
+    g1_send(2, 1)
     centre_cols(5)
     launch(5)
+    g1_wait(0, 1)
+    g2_send(0, 1)
+    hop(8, 4)
+    hop(9, 4)
+    hop(2, 2)
+    hop(4, 1)
+    g2_wait(0, 0)
     hop(3, 2)
-    g1_wait(1, 0)
-    g2_send(1, 0)
-    hop(0, 3)
-    t2_wait(1, 1)
-    g1_send(1, 1)
+    g1_wait(2, 0)
+    g2_send(2, 0)
     centre_cols(6)
     launch(6)
-    g1_wait(2, 0)
-    g2_send(2, 0)
-    hop(1, 3)
-    hop(2, 3)
-    t2_wait(2, 1)
-    g1_send(2, 1)
-    centre_cols(7)
-    launch(7)
-    hop(4, 1)
-    g1_wait(0, 1)
-    g2_send(0, 1)
     hop(5, 1)
-    hop(3, 3)
     g1_wait(1, 1)
     g2_send(1, 1)
-    hop(0, 4)
-    g2_wait(0, 0)
-    centre_cols(8)
-    launch(8)
-    hop(1, 4)
-    hop(6, 1)
-    hop(2, 4)
-    g1_wait(2, 1)
-    g2_send(2, 1)
-    centre_cols(11)
-    launch(11)
     f_wait(0, 0)
     hand_over(0)
     hand_over(1)
+    hop(2, 3)
+    g2_wait(1, 0)
+    centre_cols(7)
+    launch(7)
+    centre_cols(10)
+    launch(10)
+    hop(4, 2)
+    hop(3, 3)
+    g1_wait(2, 1)
+    g2_send(2, 1)
+    f_wait(1, 0)
+    hop(6, 1)
+    hop(5, 2)
+    g2_wait(0, 1)
+    hop(2, 4)
     hand_over(2)
-    hop(4, 2)
-    g2_wait(1, 0)
-    hop(5, 2)
+    hop(7, 1)
+    hop(10, 1)
+    f_wait(0, 1)
+    keep(0)
+    hop(4, 3)
+    keep(1)
     hop(3, 4)
     hand_over(3)
-    centre_cols(12)
-    launch(12)
-    hop(7, 1)
-    hop(8, 1)
-    f_wait(1, 0)
+    centre_cols(14)
+    launch(14)
+    g2_wait(2, 0)
+    centre_cols(11)
+    launch(11)
+    centre_cols(15)
+    launch(15)
+    hop(5, 3)
     hop(6, 2)
-    hop(11, 1)
-    g2_wait(2, 0)
-    far_send()
-    hop(4, 3)
-    hop(5, 3)
-    f_wait(2, 0)
-    hop(12, 1)
     hop(7, 2)
-    g2_wait(0, 1)
-    hop(8, 2)
-    hop(6, 3)
-    f_wait(0, 1)
-    keep(0)
-    centre_cols(10)
-    launch(10)
-    hop(11, 2)
+    hop(10, 2)
     hop(4, 4)
     hand_over(4)
+    g2_wait(1, 1)
+    hop(14, 1)
+    f_wait(2, 0)
+    keep(2)
+    hop(11, 1)
+    keep(3)
+    hop(15, 1)
+    f_wait(1, 1)
     hop(5, 4)
     hand_over(5)
-    centre_cols(13)
-    launch(13)
-    g2_wait(1, 1)
-    centre_cols(9)
-    launch(9)
+    g2_wait(2, 1)
+    hop(6, 3)
+    keep(4)
     hop(7, 3)
-    hop(12, 2)
-    keep(1)
-    hop(8, 3)
+    keep(5)
+    finish(0)
+    hop(10, 3)
+    f_wait(2, 1)
+    both(8, 12)
+    hop(14, 2)
+    both(9, 13)
+    hop(11, 2)
+    hop(15, 2)
     hop(6, 4)
     hand_over(6)
-    f_wait(1, 1)
-    g2_wait(2, 1)
-    hop(10, 1)
-    far_wait()
-    keep(2)
-    hop(11, 3)
-    keep(3)
-    keep(4)
-    centre_cols(14)
-    launch(14)
-    f_wait(2, 1)
-    hop(13, 1)
-    keep(5)
-    hop(9, 1)
-    keep(6)
     hop(7, 4)
     hand_over(7)
+    hop(10, 4)
+    keep(6)
+    hop(14, 3)
     keep(7)
-    hop(12, 3)
-    hop(8, 4)
-    hand_over(8)
-    keep(8)
-    hop(10, 2)
-    finish(0)
-    hop(11, 4)
     finish(1)
     finish(2)
+    hop(11, 3)
     finish(3)
     finish(4)
-    hop(14, 1)
-    hop(13, 2)
-    hop(9, 2)
-    hop(12, 4)
-    both(11, 12)
     finish(5)
-    hop(10, 3)
-    hop(14, 2)
-    hop(13, 3)
+    hop(15, 3)
+    hop(14, 4)
+    both(10, 14)
+    hop(11, 4)
     finish(6)
-    hop(9, 3)
-    hop(10, 4)
-    hop(14, 3)
-    hop(13, 4)
-    both(10, 13)
+    hop(15, 4)
+    both(11, 15)
     finish(7)
-    hop(9, 4)
-    hop(14, 4)
-    both(9, 14)
-    finish(8)
 
     for i in range(1, nz):
         arrive(spreads.at[(z + nz - i) % nz], pair(spread_sem, i))
@@ -519,7 +518,7 @@
     tall = 2 * rows
     wide = cols // PARTS
     piece = rows // np_
-    chunks = na * PARTS + WHOLE
+    chunks = (na + 1) * PARTS
     far = nz // 2
     dma = pltpu.SemaphoreType.DMA
     args = (col_dosage, col_ancestry, row_dosage, row_ancestry)
@@ -550,8 +549,8 @@
             pltpu.VMEM((na, nr, tall, nz * kv), BF16),
             pltpu.VMEM((tall, nz * kv), BF16),
             pltpu.VMEM((chunks, nz * kv, wide), BF16),
-            pltpu.VMEM((chunks, tall, wide), F32),
-            pltpu.VMEM((chunks, tall, wide), F32),
+            pltpu.VMEM(((na - 1) * PARTS, tall, wide), F32),
+            pltpu.VMEM(((na - 1) * PARTS, tall, wide), F32),
             dma((4,)),
             dma((2, 1)),
             dma((2, 2, nx)),
@@ -561,9 +560,9 @@
             dma((2, na, 2, 2)),
             dma((2, na, 2, nx)),
             dma((2, na, 2, nx)),
-            dma((2, 2)),
+            dma((2, PARTS, 2, far)),
             dma((2, chunks, 2, far)),
-            dma((2, chunks)),
+            dma((2, (na - 1) * PARTS)),
         ],
         compiler_params=pltpu.CompilerParams(
             collective_id=0, has_side_effects=True, vmem_limit_bytes=44 * 1024 * 1024

time: 69.9 us -> 69.1 us (0.989)
  Pallas kernels: 68.2 us -> 67 us
    pallas_call x1, Pallas kernels: 68.2 us -> 67 us  [local(): pl.pallas_call(functools.partial(kernel, sizes), out_shape=(pltpu.VMEM((n...]
where the time goes in v6:
time: 69.1 us; the launch traced here: 68.4 us
  Pallas kernels  67 us (97%)
  other arithmetic  1.4 us (2%)
    pallas_call x1, Pallas kernels, local(): pl.pallas_call(functools.partial(kernel, sizes), out_shape=(pltpu.VMEM((n...  67 us
    transpose x1, other arithmetic, local(): return jnp.transpose(total / spread[:, None, :], (1, 0, 2))  1.4 us

profile of v6, /device:TPU:1, one launch (start us, length us, event | category | flops | bytes accessed | tf_op | source)
XLA Modules:
  0.0 68.4 jit_solution(13307810892994930422)
XLA Ops:
  0.0 67.0 %shard_map.46 = (f32[3,256,512]{2,1,0:T(8,128)S(1)}, f32[3,512]{1,0:T(4,128)S(1)}) custom-call(bf16[2,256,512]{2,1,0:T(8,128)(2,1)} %cd_hbm.1, bf16[3,2,256,512]{3,2,1,0:T(8,128)(2,1)} %ca_hbm.1, bf16[2,256,128]{2,1,0:T(8,128)(2,1)} %rd_hbm.1, bf16[3,2,256,128]{3,2,1,0:T(8,128)(2,1)} %ra_hbm.1), custom_call_target="tpu_custom_call" | custom-call | tf_op jit(solution)/shard_map/pallas_call | solution.py:526
  67.0 1.4 %divide_bitcast_fusion = f32[256,3,512]{2,0,1:T(8,128)} fusion(f32[3,256,512]{2,1,0:T(8,128)S(1)} %get-tuple-element.7, f32[3,512]{1,0:T(4,128)S(1)} %get-tuple-element.8), kind=kLoop, calls=%fused_computation | loop fusion | flops 393216 | bytes 3151872 | tf_op jit(solution)/shard_map/transpose | solution.py:571

commit v7 on v6

--- a/solution.py
+++ b/solution.py
@@ -155,10 +155,10 @@
 
     arrive(part.at[1 - c], pair(pair_sem, 0))
     stat[p] = part[0] + part[1]
-    for i in range(1, nx):
-        push(stat.at[p], stat.at[p], pair(stat_sem, 0, i), device(chip(((x + i) % nx) * 2 + h), z, r))
-    for i in range(nx):
+    for i in sorted(range(nx), key=lambda i: -min(i, nx - i)):
         push(stat.at[p], stat.at[p], pair(stat_sem, 1, i), device(chip(((x + i) % nx) * 2 + 1 - h), z, other))
+        if i:
+            push(stat.at[p], stat.at[p], pair(stat_sem, 0, i), device(chip(((x + i) % nx) * 2 + h), z, r))
 
     kinds = (pl.ds(0, 4), pl.ds(4, 2 * na - 2))
 
@@ -203,7 +203,7 @@
         return hold.at[a, o, :, pl.ds(aligned(zz * kv, kv), kv)]
 
     def t2_send(a, o):
-        for i in range(1, nz):
+        for i in sorted(range(1, nz), key=lambda i: -min(i, nz - i)):
             to = (z + i) % nz
             push(centred.at[a, o, to], hold_from(a, o, z), pair(t2_sem, a, o, i), device(s, to, r))
 
@@ -234,7 +234,7 @@
 
     def g2_send(a, o):
         ref = a_rows(a, o, c, x * 2, 2)
-        for i in range(1, nx):
+        for i in sorted(range(1, nx), key=lambda i: -min(i, nx - i)):
             push(ref, ref, pair(g2_sem, a, o, i), device(chip(((x + i) % nx) * 2 + h), z, r))
         push(ref, ref, pair(f_sem, a, o, 0), sibling)
 

time: 69.1 us -> 68.8 us (level)
  no operation moved by 1% of the time
where the time goes in v7:
time: 68.8 us; the launch traced here: 68.4 us
  Pallas kernels  67 us (97%)
  other arithmetic  1.4 us (2%)
    pallas_call x1, Pallas kernels, local(): pl.pallas_call(functools.partial(kernel, sizes), out_shape=(pltpu.VMEM((n...  67 us
    transpose x1, other arithmetic, local(): return jnp.transpose(total / spread[:, None, :], (1, 0, 2))  1.4 us

profile of v7, /device:TPU:1, one launch (start us, length us, event | category | flops | bytes accessed | tf_op | source)
XLA Modules:
  0.0 68.4 jit_solution(1633166610575585427)
XLA Ops:
  0.0 67.0 %shard_map.46 = (f32[3,256,512]{2,1,0:T(8,128)S(1)}, f32[3,512]{1,0:T(4,128)S(1)}) custom-call(bf16[2,256,512]{2,1,0:T(8,128)(2,1)} %cd_hbm.1, bf16[3,2,256,512]{3,2,1,0:T(8,128)(2,1)} %ca_hbm.1, bf16[2,256,128]{2,1,0:T(8,128)(2,1)} %rd_hbm.1, bf16[3,2,256,128]{3,2,1,0:T(8,128)(2,1)} %ra_hbm.1), custom_call_target="tpu_custom_call" | custom-call | tf_op jit(solution)/shard_map/pallas_call | solution.py:526
  67.0 1.4 %divide_bitcast_fusion = f32[256,3,512]{2,0,1:T(8,128)} fusion(f32[3,256,512]{2,1,0:T(8,128)S(1)} %get-tuple-element.7, f32[3,512]{1,0:T(4,128)S(1)} %get-tuple-element.8), kind=kLoop, calls=%fused_computation | loop fusion | flops 393216 | bytes 3151872 | tf_op jit(solution)/shard_map/transpose | solution.py:571
